TPU v7x, 32 devices: a whole 2x2x4 slice. The times are simulated.
32 devices in a mesh: sx: 4 (over y, core), sy: 8 (over z, x).
Axes of the slice: x: 2, y: 2, z: 4, core: 2. Of those that a mesh axis runs over, the one named last changes fastest.
Arguments:
- skip_features: bfloat16 [1024, 64, 128], P(('sx', 'sy')), may hold values from -6 to 6
- coarse_features: bfloat16 [256, 64, 128], P(('sx', 'sy')), may hold values from -6 to 6
- child_code: int32 [1024], P(('sx', 'sy')), may hold values from 0 to 63
- neighbours: int32 [1024, 27], P(('sx', 'sy')), may hold values from -1 to 71, as said below
- send_face: int32 [32, 4, 8], P(('sx', 'sy')), may hold values from 0 to 31, as said below
- send_corner: int32 [32, 4, 2], P(('sx', 'sy')), may hold values from 0 to 31, as said below
- live_count: int32 [32], P(('sx', 'sy')), may hold values from 8 to 32, as said below
- weight: bfloat16 [27, 128, 128], replicated, may hold values from -0.109375 to 0.109375
- conv_bias: float32 [128], replicated, may hold values from -3 to 3
- cotangent: bfloat16 [1024, 64, 128], P(('sx', 'sy')), may hold values from -6 to 6
Outputs:
- activated: bfloat16 [1024, 64, 128], P(('sx', 'sy'))
- skip_grad: bfloat16 [1024, 64, 128], P(('sx', 'sy'))
- coarse_grad: bfloat16 [256, 64, 128], P(('sx', 'sy'))
- weight_grad: float32 [27, 128, 128], replicated
- bias_grad: float32 [128], replicated
Inputs may be any that keep to these rules, and one draw needn't show every extreme that they name: `live_count`: one device has all 32 slots live; slots from the count on are empty. `send_face`: slots of live bricks of the sending device, distinct within one list. `send_corner`: slots of live bricks of the sending device, distinct within one list. `neighbours`: for a live slot, entries below 32 name live slots of the same device; offset 13 names the slot itself.
All inputs are finite; a program needn't handle non-finite values.
Results may differ from a plain program's by a relative error of at most 0.0056.
Values may be sent and summed in bfloat16 or wider, within the bound.
A program may use at most 128 MiB of HBM per device.

v0:
```python
import jax
import jax.numpy as jnp
from jax import lax
from jax.sharding import PartitionSpec as P

SOURCE_SPANS = ((3, 4), (0, 4), (0, 1))
TARGET_SPANS = ((0, 1), (1, 5), (5, 6))


def from_behind(block, axis, distance):
    devices = range(lax.axis_size(axis))
    route = [(i - distance, i) for i in devices if i - distance in devices]
    return lax.ppermute(block, axis, route)


def voxel_table():
    voxel_ids = jnp.arange(64, dtype=jnp.int32)
    octant = jnp.arange(8, dtype=jnp.int32)
    coord_x = voxel_ids // 16
    coord_y = voxel_ids // 4 % 4
    coord_z = voxel_ids % 4
    half_x = octant // 4
    half_y = octant // 2 % 2
    half_z = octant % 2
    return (
        (2 * half_x[:, None] + coord_x[None, :] // 2) * 16
        + (2 * half_y[:, None] + coord_y[None, :] // 2) * 4
        + (2 * half_z[:, None] + coord_z[None, :] // 2)
    )


def padded_block(gathered, channels):
    brick_count = gathered.shape[0]
    shaped = gathered.reshape(brick_count, 27, 4, 4, 4, channels)
    planes = []
    for along_x in range(3):
        line_list = []
        for along_y in range(3):
            cell_list = []
            for along_z in range(3):
                offset = along_x * 9 + along_y * 3 + along_z
                span_x = SOURCE_SPANS[along_x]
                span_y = SOURCE_SPANS[along_y]
                span_z = SOURCE_SPANS[along_z]
                cell_list.append(
                    shaped[
                        :,
                        offset,
                        span_x[0] : span_x[1],
                        span_y[0] : span_y[1],
                        span_z[0] : span_z[1],
                        :,
                    ]
                )
            line_list.append(jnp.concatenate(cell_list, axis=3))
        planes.append(jnp.concatenate(line_list, axis=2))
    return jnp.concatenate(planes, axis=1)


def unfold_taps(padded, channels):
    brick_count = padded.shape[0]
    tap_list = []
    for tap_x in range(3):
        for tap_y in range(3):
            for tap_z in range(3):
                tap_list.append(
                    padded[:, tap_x : tap_x + 4, tap_y : tap_y + 4, tap_z : tap_z + 4, :]
                )
    return jnp.concatenate(tap_list, axis=-1).reshape(brick_count * 64, 27 * channels)


def fold_taps(grad_cols, brick_count, channels):
    shaped = grad_cols.reshape(brick_count, 4, 4, 4, 27, channels)
    grad_pad = jnp.zeros((brick_count, 6, 6, 6, channels), jnp.float32)
    for tap_x in range(3):
        for tap_y in range(3):
            for tap_z in range(3):
                tap_id = tap_x * 9 + tap_y * 3 + tap_z
                grad_pad = grad_pad.at[
                    :, tap_x : tap_x + 4, tap_y : tap_y + 4, tap_z : tap_z + 4, :
                ].add(shaped[:, :, :, :, tap_id, :])
    pieces = []
    for along_x in range(3):
        for along_y in range(3):
            for along_z in range(3):
                target_x = TARGET_SPANS[along_x]
                target_y = TARGET_SPANS[along_y]
                target_z = TARGET_SPANS[along_z]
                span_x = SOURCE_SPANS[along_x]
                span_y = SOURCE_SPANS[along_y]
                span_z = SOURCE_SPANS[along_z]
                inner_part = grad_pad[
                    :,
                    target_x[0] : target_x[1],
                    target_y[0] : target_y[1],
                    target_z[0] : target_z[1],
                    :,
                ]
                pieces.append(
                    jnp.pad(
                        inner_part,
                        (
                            (0, 0),
                            (span_x[0], 4 - span_x[1]),
                            (span_y[0], 4 - span_y[1]),
                            (span_z[0], 4 - span_z[1]),
                            (0, 0),
                        ),
                    )
                )
    return jnp.stack(pieces, axis=1).reshape(brick_count, 27, 64, channels)


def cross_x(face_piece, corner_pair, step_sign):
    face_moved = from_behind(face_piece, "sx", step_sign)
    corner_moved = from_behind(corner_pair, "sx", step_sign)
    return (face_moved, corner_moved)


def cross_y(face_piece, corner_pair, step_sign):
    face_moved = from_behind(face_piece, "sy", step_sign)
    corner_moved = from_behind(corner_pair, "sy", step_sign)
    return (face_moved, corner_moved)


def return_y(face_piece, corner_pair, step_sign):
    face_moved = from_behind(face_piece.astype(jnp.bfloat16), "sy", step_sign).astype(
        face_piece.dtype
    )
    corner_moved = from_behind(corner_pair.astype(jnp.bfloat16), "sy", step_sign).astype(
        corner_pair.dtype
    )
    return (face_moved, corner_moved)


def return_x(face_piece, corner_pair, step_sign):
    face_moved = from_behind(face_piece.astype(jnp.bfloat16), "sx", step_sign).astype(
        face_piece.dtype
    )
    corner_moved = from_behind(corner_pair.astype(jnp.bfloat16), "sx", step_sign).astype(
        corner_pair.dtype
    )
    return (face_moved, corner_moved)


def forward_route(face_rows, corner_rows):
    received = []
    for step_sign in (1, -1):
        lane_id = 0 if step_sign == 1 else 1
        received.append(
            cross_x(face_rows[lane_id], corner_rows[2 * lane_id : 2 * lane_id + 2], step_sign)
        )
    face_low, corners_low = received[0]
    face_high, corners_high = received[1]
    onward = []
    for step_sign in (1, -1):
        lane_id = 0 if step_sign == 1 else 1
        corner_pair = jnp.stack([corners_low[lane_id], corners_high[lane_id]])
        onward.append(cross_y(face_rows[2 + lane_id], corner_pair, step_sign))
    face_left, corners_left = onward[0]
    face_right, corners_right = onward[1]
    face_groups = jnp.stack([face_low, face_high, face_left, face_right])
    corner_groups = jnp.stack(
        [corners_left[0], corners_right[0], corners_left[1], corners_right[1]]
    )
    return (face_groups, corner_groups)


def backward_route(face_part, corner_part):
    returned = []
    for step_sign in (-1, 1):
        lane_id = 0 if step_sign == -1 else 1
        corner_pair = jnp.stack([corner_part[lane_id], corner_part[2 + lane_id]])
        returned.append(return_y(face_part[2 + lane_id], corner_pair, step_sign))
    face_plus_y, corners_plus_y = returned[0]
    face_minus_y, corners_minus_y = returned[1]
    homeward = []
    for step_sign in (-1, 1):
        lane_id = 0 if step_sign == -1 else 1
        corner_pair = jnp.stack([corners_plus_y[lane_id], corners_minus_y[lane_id]])
        homeward.append(return_x(face_part[lane_id], corner_pair, step_sign))
    face_first, corners_first = homeward[0]
    face_second, corners_second = homeward[1]
    face_back = jnp.stack([face_first, face_second, face_plus_y, face_minus_y])
    corner_back = jnp.concatenate([corners_first, corners_second], axis=0)
    return (face_back, corner_back)


def reduce_kernel(weight_sum, bias_sum):
    weight_total, bias_total = lax.psum((weight_sum, bias_sum), ("sx", "sy"))
    return (weight_total, bias_total)


def local(
    skip_features,
    coarse_features,
    child_code,
    neighbours,
    send_face,
    send_corner,
    live_count,
    weight,
    conv_bias,
    cotangent,
):
    bricks = skip_features.shape[0]
    channels = skip_features.shape[2]
    parents = coarse_features.shape[0]
    face_cap = send_face.shape[2]
    corner_cap = send_corner.shape[2]
    live_total = live_count[0]
    slot_live = (jnp.arange(bricks, dtype=jnp.int32) < live_total).astype(jnp.float32)
    row_index = (child_code // 8)[:, None] * 64 + voxel_table()[child_code % 8]
    coarse_rows = coarse_features.reshape(parents * 64, channels)
    upsampled = jnp.take(coarse_rows, row_index, axis=0)
    hidden = (
        (skip_features.astype(jnp.float32) + upsampled.astype(jnp.float32))
        * slot_live[:, None, None]
    ).astype(jnp.bfloat16)
    face_rows = jnp.take(hidden, send_face[0], axis=0)
    corner_rows = jnp.take(hidden, send_corner[0], axis=0)
    face_groups, corner_groups = forward_route(face_rows, corner_rows)
    brick_table = jnp.concatenate(
        [
            hidden,
            face_groups.reshape(-1, 64, channels),
            corner_groups.reshape(-1, 64, channels),
            jnp.zeros((1, 64, channels), jnp.bfloat16),
        ],
        axis=0,
    )
    sentinel = brick_table.shape[0] - 1
    lookup = jnp.where(neighbours < 0, sentinel, neighbours)
    flat_weight = weight.reshape(27 * channels, channels)
    block_size = min(16, bricks)

    def block_step(block_index, state_now):
        outputs, table_grad, weight_sum, bias_sum = state_now
        first_slot = block_index * block_size
        slot_ids = lax.dynamic_slice_in_dim(lookup, first_slot, block_size, 0)
        gathered = jnp.take(brick_table, slot_ids, axis=0)
        columns = unfold_taps(padded_block(gathered, channels), channels)
        pre_act = jnp.dot(columns, flat_weight, preferred_element_type=jnp.float32) + conv_bias
        keep_rows = jnp.repeat(lax.dynamic_slice_in_dim(slot_live, first_slot, block_size, 0), 64)[
            :, None
        ]
        sigmoid_value = jax.nn.sigmoid(pre_act)
        result = (pre_act * sigmoid_value * keep_rows).astype(jnp.bfloat16)
        upstream = lax.dynamic_slice_in_dim(cotangent, first_slot, block_size, 0).reshape(
            block_size * 64, channels
        )
        grad_pre = (
            upstream.astype(jnp.float32)
            * sigmoid_value
            * (1.0 + pre_act * (1.0 - sigmoid_value))
            * keep_rows
        ).astype(jnp.bfloat16)
        weight_sum = weight_sum + lax.dot_general(
            columns, grad_pre, (((0,), (0,)), ((), ())), preferred_element_type=jnp.float32
        )
        bias_sum = bias_sum + jnp.sum(grad_pre.astype(jnp.float32), axis=0)
        grad_cols = lax.dot_general(
            grad_pre, flat_weight, (((1,), (1,)), ((), ())), preferred_element_type=jnp.float32
        )
        pieces = fold_taps(grad_cols, block_size, channels)
        table_grad = table_grad.at[slot_ids.reshape(-1)].add(pieces.reshape(-1, 64, channels))
        outputs = lax.dynamic_update_slice_in_dim(
            outputs, result.reshape(block_size, 64, channels), first_slot, 0
        )
        return (outputs, table_grad, weight_sum, bias_sum)

    initial = (
        jnp.zeros((bricks, 64, channels), jnp.bfloat16),
        jnp.zeros((brick_table.shape[0], 64, channels), jnp.float32),
        jnp.zeros((27 * channels, channels), jnp.float32),
        jnp.zeros((channels,), jnp.float32),
    )
    block_total = (live_total + block_size - 1) // block_size
    outputs, table_grad, weight_sum, bias_sum = lax.fori_loop(0, block_total, block_step, initial)
    local_grad = table_grad[:bricks]
    face_part = table_grad[bricks : bricks + 4 * face_cap].reshape(4, face_cap, 64, channels)
    corner_part = table_grad[
        bricks + 4 * face_cap : bricks + 4 * face_cap + 4 * corner_cap
    ].reshape(4, corner_cap, 64, channels)
    face_back, corner_back = backward_route(face_part, corner_part)
    local_grad = local_grad.at[send_face[0].reshape(-1)].add(face_back.reshape(-1, 64, channels))
    local_grad = local_grad.at[send_corner[0].reshape(-1)].add(
        corner_back.reshape(-1, 64, channels)
    )
    coarse_sum = (
        jnp.zeros((parents * 64, channels), jnp.float32)
        .at[row_index.reshape(-1)]
        .add(local_grad.reshape(-1, channels))
    )
    weight_total, bias_total = reduce_kernel(weight_sum, bias_sum)
    return (
        outputs,
        local_grad.astype(jnp.bfloat16),
        coarse_sum.reshape(parents, 64, channels).astype(jnp.bfloat16),
        weight_total.reshape(27, channels, channels),
        bias_total,
    )


def solution(mesh):
    placed = (
        P(("sx", "sy"), None, None),
        P(("sx", "sy"), None, None),
        P(("sx", "sy")),
        P(("sx", "sy"), None),
        P(("sx", "sy"), None, None),
        P(("sx", "sy"), None, None),
        P(("sx", "sy")),
        P(),
        P(),
        P(("sx", "sy"), None, None),
    )
    return jax.shard_map(
        local,
        mesh=mesh,
        in_specs=placed,
        out_specs=(
            P(("sx", "sy"), None, None),
            P(("sx", "sy"), None, None),
            P(("sx", "sy"), None, None),
            P(),
            P(),
        ),
        check_vma=False,
    )
```

profile of v0, /device:TPU:1, one launch (start us, length us, event | category | flops | bytes accessed | tf_op | source)
XLA Modules:
  0.0 922.2 jit_solution(12983260083366345)
XLA Ops:
  57.5 362.9 %while.46 = (s32[]{:T(128)}, bf16[32,64,128]{2,1,0:T(8,128)(2,1)}, f32[73,64,128]{2,1,0:T(8,128)}, f32[3456,128]{1,0:T(8,128)}, f32[128]{0:T(128)S(1)}, /*index=...) while((s32[]{:T(128)}, bf16[32,64,128]{2,1,0:T(8,128)(2,1)}, ...), condition=%wide.region_3.4_spmd, body=%wide.region_0.3_spmd.sunk | while | flops 2756130816 | bytes 327153472 | solution.py:279
  60.6 21.0 %gather_fusion = bf16[432,64,128]{2,1,0:T(8,128)(2,1)} fusion(bf16[73,64,128]{2,1,0:T(8,128)(2,1)} %get-tuple-element.1177, s32[1024]{0:T(1024)S(1)} %pad_clamp_fusion.5), kind=kCustom, calls=%fused_computation.clone.1 | custom fusion | bytes 14157504 | tf_op jit(solution)/shard_map/while/body/jit(_take)/gather | solution.py:241
  81.6 9.4 %broadcast_select_fusion.4 = bf16[16,27,4,4,4,128]{5,4,3,2,1,0:T(4,128)(2,1)} fusion(bf16[16,27,4,4,4,128]{5,4,3,2,1,0:T(4,128)(2,1)} %bitcast.533, pred[16,27]{1,0:T(8,128)(4,1)S(1)} %get-tuple-element.1009), kind=kLoop, calls=%fused_computation.9.clone.1 | loop fusion | flops 3538944 | bytes 14156208 | tf_op jit(solution)/shard_map/while/body/jit(_take)/select_n | solution.py:241
  118.0 8.2 fusion.106
  126.2 16.5 %reshape.2247 = f32[16,4,4,4,27,128]{5,4,3,2,1,0:T(8,128)} reshape(f32[1024,3456]{1,0:T(8,128)} %fusion.106) | data formatting | bytes 28311552 | tf_op jit(solution)/shard_map/while/body/reshape | solution.py:73
  142.8 15.7 %fusion.107 = (f32[16,4,4,4,1,128]{5,4,3,2,1,0:T(1,128)S(1)}, f32[16,4,4,4,1,128]{5,4,3,2,1,0:T(1,128)}, f32[16,4,4,4,1,128]{5,4,3,2,1,0:T(1,128)}, f32[16,4,4,4...) fusion(f32[16,4,4,4,27,128]{5,4,3,2,1,0:T(8,128)} %reshape.2247), kind=kLoop, calls=%fused_computation.248.clone.1 | loop fusion | bytes 8388608 | tf_op jit(solution)/shard_map/while/body/slice | solution.py:81
  158.5 32.5 %fusion.112 = (f32[16,4,4,4,1,128]{5,4,3,2,1,0:T(1,128)S(1)}, f32[16,4,4,4,1,128]{5,4,3,2,1,0:T(1,128)}, f32[16,4,4,4,1,128]{5,4,3,2,1,0:T(1,128)}, f32[16,4,4,4...) fusion(f32[16,4,4,4,27,128]{5,4,3,2,1,0:T(8,128)} %reshape.2247), kind=kLoop, calls=%fused_computation.247.clone.1 | loop fusion | bytes 19922944 | tf_op jit(solution)/shard_map/while/body/slice | solution.py:81
  192.3 6.7 scatter-add.226
  201.0 6.7 scatter-add.227
  211.1 6.7 scatter-add.228
  221.6 8.6 scatter-add.229
  252.3 6.7 scatter-add.232
  261.0 6.9 scatter-add.233
  271.2 6.7 scatter-add.234
  289.9 6.7 scatter-add.236
  298.6 6.7 scatter-add.237
  308.6 6.7 scatter-add.238
  336.0 6.7 scatter-add.241
  345.0 6.7 scatter-add.242
  362.2 6.9 copy.250
  369.1 44.5 %scatter_fusion = f32[73,64,128]{2,1,0:T(8,128)S(1)} fusion(f32[73,64,128]{2,1,0:T(8,128)S(1)} %copy-done.2, s32[432]{0:T(512)S(1)} %bitcast.596, f32[432,64,128]{2,1,0:T(8,128)} %bitcast.532), kind=kCustom, calls=%fused_computation.5.clone.1 | custom fusion | flops 3538944 | bytes 42469056 | tf_op jit(solution)/shard_map/while/body/scatter-add | solution.py:266
  437.8 396.6 %psum.15 = f32[128]{0:T(128)} all-reduce(f32[128]{0:T(128)S(1)} %get-tuple-element.623), channel_id=1, replica_groups=mesh['sx'=4,'sy'=8] {'sx','sy'}, use_global_device_ids=true, to_apply=%region_8.9 | all-reduce | flops 128 | bytes 1024 | tf_op jit(solution)/shard_map/psum | solution.py:190
  849.1 11.7 %scatter_custom_fusion.3 = f32[512,128]{1,0:T(8,128)S(1)} fusion(s32[2048]{0:T(1024)} %bitcast.606, f32[2048,128]{1,0:T(8,128)S(1)} %bitcast.589, f32[]{:T(128)} %constant.1250.clone.1), kind=kCustom, calls=%fused_computation.165 | custom fusion | flops 262144 | bytes 262656 | tf_op jit(solution)/shard_map/scatter-add | solution.py:293
  861.5 50.9 %all-reduce.29.cloned.1.call-done = f32[27,128,128]{2,1,0:T(8,128)} async-done(((f32[27,128,128]{2,1,0:T(8,128)}), f32[27,128,128]{2,1,0:T(8,128)}) %all-reduce.29.cloned.1.call-update) | async-done | bytes 1769488 | tf_op jit(solution)/shard_map/psum | solution.py:190
  (271 shorter events, 204.1 us)
Async XLA Ops:
  7.2 28.8 %copy-start.6 = (s32[1,4,2]{1,2,0:T(2,128)S(1)}, s32[1,4,2]{1,2,0:T(2,128)}, u32[]{:S(2)}) copy-start(s32[1,4,2]{1,2,0:T(2,128)} %param.71) | copy-start | bytes 100
  7.2 18.8 %copy-start.4 = (s32[1,4,8]{2,1,0:T(4,128)S(1)}, s32[1,4,8]{2,1,0:T(4,128)}, u32[]{:S(2)}) copy-start(s32[1,4,8]{2,1,0:T(4,128)} %param.70) | copy-start | bytes 388
  7.2 30.2 %copy-start.5 = (s32[32,27]{1,0:T(8,128)S(1)}, s32[32,27]{1,0:T(8,128)}, u32[]{:S(2)}) copy-start(s32[32,27]{1,0:T(8,128)} %param.69) | copy-start | bytes 10372
  7.2 905.1 %all-reduce.29.cloned.1.call-start = ((), (), s32[]{:S(2)}) async-start(), calls=%async_computation | async-start | bytes 3538944 | tf_op jit(solution)/shard_map/psum | solution.py:190
  17.4 40.1 %copy-start.9 = (f32[128]{0:T(128)S(1)}, f32[128]{0:T(128)}, u32[]{:S(2)}) copy-start(f32[128]{0:T(128)} %param.74) | copy-start | bytes 1540
  19.5 19.2 %collective-permute-start.4 = (bf16[2,2,64,128]{3,2,1,0:T(8,128)(2,1)S(1)}, bf16[2,2,64,128]{3,2,1,0:T(8,128)(2,1)S(1)}, u32[]{:S(2)}, u32[]{:S(2)}) collective-permute-start(bf16[2,2,64,128]{3,2,1,0:T(8,128)(2,1)S(1)} %get-tuple-element.788), channel_id=1, source_target_pairs={{0,8},{8,16},{16,24},{1,9},{9,17},{17,25},{2,10},{10,18},{18,26},{... | collective-permute-start | bytes 196616 | tf_op jit(solution)/shard_map/ppermute | solution.py:13
  24.1 16.6 %collective-permute-start.5 = (bf16[2,2,64,128]{3,2,1,0:T(8,128)(2,1)S(1)}, bf16[2,2,64,128]{3,2,1,0:T(8,128)(2,1)S(1)}, u32[]{:S(2)}, u32[]{:S(2)}) collective-permute-start(bf16[2,2,64,128]{3,2,1,0:T(8,128)(2,1)S(1)} %get-tuple-element.789), channel_id=1, source_target_pairs={{8,0},{16,8},{24,16},{9,1},{17,9},{25,17},{10,2},{18,10},{26,18},{... | collective-permute-start | bytes 196616 | tf_op jit(solution)/shard_map/ppermute | solution.py:13
  27.0 25.3 %collective-permute-start = (bf16[8,64,128]{2,1,0:T(8,128)(2,1)S(1)}, bf16[8,64,128]{2,1,0:T(8,128)(2,1)S(1)}, u32[]{:S(2)}, u32[]{:S(2)}) collective-permute-start(bf16[8,64,128]{2,1,0:T(8,128)(2,1)S(1)} %get-tuple-element.784), channel_id=1, source_target_pairs={{0,8},{8,16},{16,24},{1,9},{9,17},{17,25},{2,10},{10,18},{18,26},{... | collective-permute-start | bytes 393224 | tf_op jit(solution)/shard_map/ppermute | solution.py:13
  30.6 21.6 %collective-permute-start.3 = (bf16[8,64,128]{2,1,0:T(8,128)(2,1)S(1)}, bf16[8,64,128]{2,1,0:T(8,128)(2,1)S(1)}, u32[]{:S(2)}, u32[]{:S(2)}) collective-permute-start(bf16[8,64,128]{2,1,0:T(8,128)(2,1)S(1)} %get-tuple-element.785), channel_id=1, source_target_pairs={{1,0},{2,1},{3,2},{4,3},{5,4},{6,5},{7,6},{9,8},{10,9},{11,10},{12... | collective-permute-start | bytes 393224 | tf_op jit(solution)/shard_map/ppermute | solution.py:13
  31.9 20.3 %collective-permute-start.2 = (bf16[8,64,128]{2,1,0:T(8,128)(2,1)S(1)}, bf16[8,64,128]{2,1,0:T(8,128)(2,1)S(1)}, u32[]{:S(2)}, u32[]{:S(2)}) collective-permute-start(bf16[8,64,128]{2,1,0:T(8,128)(2,1)S(1)} %get-tuple-element.786), channel_id=1, source_target_pairs={{0,1},{1,2},{2,3},{3,4},{4,5},{5,6},{6,7},{8,9},{9,10},{10,11},{11... | collective-permute-start | bytes 393224 | tf_op jit(solution)/shard_map/ppermute | solution.py:13
  38.7 13.5 %collective-permute-start.1 = (bf16[8,64,128]{2,1,0:T(8,128)(2,1)S(1)}, bf16[8,64,128]{2,1,0:T(8,128)(2,1)S(1)}, u32[]{:S(2)}, u32[]{:S(2)}) collective-permute-start(bf16[8,64,128]{2,1,0:T(8,128)(2,1)S(1)} %get-tuple-element.787), channel_id=1, source_target_pairs={{8,0},{16,8},{24,16},{9,1},{17,9},{25,17},{10,2},{18,10},{26,18},{... | collective-permute-start | bytes 393224 | tf_op jit(solution)/shard_map/ppermute | solution.py:13
  40.7 5.7 collective-permute-start.7
  46.4 5.8 collective-permute-start.6
  420.4 424.0 %copy-start.8 = (s32[32]{0:T(128)S(1)}, s32[32]{0:T(128)}, u32[]{:S(2)}) copy-start(s32[32]{0:T(128)} %fusion.20) | copy-start | bytes 388
  421.7 425.7 %copy-start.7 = (s32[8]{0:T(128)S(1)}, s32[8]{0:T(128)}, u32[]{:S(2)}) copy-start(s32[8]{0:T(128)} %fusion.21) | copy-start | bytes 100
  423.7 491.5 %copy-start.1 = (bf16[8,64,128]{2,1,0:T(8,128)(2,1)S(1)}, bf16[8,64,128]{2,1,0:T(8,128)(2,1)}, u32[]{:S(2)}) copy-start(bf16[8,64,128]{2,1,0:T(8,128)(2,1)} %param.67) | copy-start | bytes 393220
  423.7 410.7 %collective-permute-start.13 = (bf16[2,2,64,128]{3,2,1,0:T(8,128)(2,1)S(1)}, bf16[2,2,64,128]{3,2,1,0:T(8,128)(2,1)S(1)}, u32[]{:S(2)}, u32[]{:S(2)}) collective-permute-start(bf16[2,2,64,128]{3,2,1,0:T(8,128)(2,1)S(1)} %pad_maximum_fusion.11), channel_id=1, source_target_pairs={{0,1},{1,2},{2,3},{3,4},{4,5},{5,6},{6,7},{8,9},{9,10},{10,11},{11... | collective-permute-start | bytes 196616 | tf_op jit(solution)/shard_map/ppermute | solution.py:13
  428.0 411.7 %collective-permute-start.12 = (bf16[2,2,64,128]{3,2,1,0:T(8,128)(2,1)S(1)}, bf16[2,2,64,128]{3,2,1,0:T(8,128)(2,1)S(1)}, u32[]{:S(2)}, u32[]{:S(2)}) collective-permute-start(bf16[2,2,64,128]{3,2,1,0:T(8,128)(2,1)S(1)} %pad_maximum_fusion.10), channel_id=1, source_target_pairs={{1,0},{2,1},{3,2},{4,3},{5,4},{6,5},{7,6},{9,8},{10,9},{11,10},{12... | collective-permute-start | bytes 196616 | tf_op jit(solution)/shard_map/ppermute | solution.py:13
  429.3 412.4 %collective-permute-start.8 = (bf16[8,64,128]{2,1,0:T(8,128)(2,1)S(1)}, bf16[8,64,128]{2,1,0:T(8,128)(2,1)S(1)}, u32[]{:S(2)}, u32[]{:S(2)}) collective-permute-start(bf16[8,64,128]{2,1,0:T(8,128)(2,1)S(1)} %get-tuple-element.780), channel_id=1, source_target_pairs={{8,0},{16,8},{24,16},{9,1},{17,9},{25,17},{10,2},{18,10},{26,18},{... | collective-permute-start | bytes 393224 | tf_op jit(solution)/shard_map/ppermute | solution.py:13
  432.2 411.9 %collective-permute-start.11 = (bf16[8,64,128]{2,1,0:T(8,128)(2,1)S(1)}, bf16[8,64,128]{2,1,0:T(8,128)(2,1)S(1)}, u32[]{:S(2)}, u32[]{:S(2)}) collective-permute-start(bf16[8,64,128]{2,1,0:T(8,128)(2,1)S(1)} %get-tuple-element.781), channel_id=1, source_target_pairs={{0,1},{1,2},{2,3},{3,4},{4,5},{5,6},{6,7},{8,9},{9,10},{10,11},{11... | collective-permute-start | bytes 393224 | tf_op jit(solution)/shard_map/ppermute | solution.py:13
  436.5 407.6 %collective-permute-start.10 = (bf16[8,64,128]{2,1,0:T(8,128)(2,1)S(1)}, bf16[8,64,128]{2,1,0:T(8,128)(2,1)S(1)}, u32[]{:S(2)}, u32[]{:S(2)}) collective-permute-start(bf16[8,64,128]{2,1,0:T(8,128)(2,1)S(1)} %get-tuple-element.782), channel_id=1, source_target_pairs={{1,0},{2,1},{3,2},{4,3},{5,4},{6,5},{7,6},{9,8},{10,9},{11,10},{12... | collective-permute-start | bytes 393224 | tf_op jit(solution)/shard_map/ppermute | solution.py:13
  834.4 9.7 %collective-permute-start.9 = (bf16[8,64,128]{2,1,0:T(8,128)(2,1)S(1)}, bf16[8,64,128]{2,1,0:T(8,128)(2,1)S(1)}, u32[]{:S(2)}, u32[]{:S(2)}) collective-permute-start(bf16[8,64,128]{2,1,0:T(8,128)(2,1)S(1)} %get-tuple-element.783), channel_id=1, source_target_pairs={{0,8},{8,16},{16,24},{1,9},{9,17},{17,25},{2,10},{10,18},{18,26},{... | collective-permute-start | bytes 393224 | tf_op jit(solution)/shard_map/ppermute | solution.py:13
  839.7 6.8 collective-permute-start.15
  841.7 5.6 collective-permute-start.14
  (3 other events, 12.4 us)
Sparse Core Ops, SparseCore 0:
  423.8 488.4 all-reduce.28
where the time goes:
time: 937 us; the launch traced here: 922 us
  blocking collectives  397 us (42%)
  local copies, waits for them, and re-layouts  253 us (27%)
  other arithmetic  130 us (14%)
  waiting for transfers between devices  57.6 us (6%)
  starting transfers between devices  46.5 us (5%)
  matrix products  16.4 us (2%)
  between operations  15.5 us (2%)
    psum x1, blocking collectives, reduce_kernel(): weight_total, bias_total = lax.psum((weight_sum, bias_sum), ('sx', 'sy'))  397 us
    scatter-add x19, local copies, waits for them, and re-layouts, fold_taps(): grad_pad = grad_pad.at[:, tap_x:tap_x + 4, tap_y:tap_y + 4, tap_z:tap_z +...  121 us
    psum x1, waiting for transfers between devices, reduce_kernel(): weight_total, bias_total = lax.psum((weight_sum, bias_sum), ('sx', 'sy'))  50.9 us
    slice x2, local copies, waits for them, and re-layouts, fold_taps(): shaped[:, :, :, :, tap_id, :]  48.2 us
    ppermute x16, starting transfers between devices, from_behind(): return lax.ppermute(block, axis, route)  46.4 us
    scatter-add x1, other arithmetic, block_step(): table_grad.at[slot_ids.reshape(-1)].add(pieces.reshape(-1, 64, channels))  44.5 us
    add x18, other arithmetic, fold_taps(): grad_pad = grad_pad.at[:, tap_x:tap_x + 4, tap_y:tap_y + 4, tap_z:tap_z +...  34.8 us
    gather x1, local copies, waits for them, and re-layouts, block_step(): gathered = jnp.take(brick_table, slot_ids, axis=0)  21 us
  transfers between devices with their start and end apart: 17, of which 4 were waited for; matrix products, arithmetic and copies ran while one was open for 2% of the time, Pallas kernels for 0%

commit v1 on v0

v1 whole, which is shorter than its diff:
```python
import functools

import jax
import jax.numpy as jnp
from jax import lax
from jax.experimental import pallas as pl
from jax.experimental.pallas import tpu as pltpu
from jax.sharding import PartitionSpec as P

F32 = jnp.float32
BF16 = jnp.bfloat16
C = 128
STEPS = ((1, 0), (-1, 0), (0, 1), (0, -1), (1, 1), (1, -1), (-1, 1), (-1, -1))


def sources():
    def along(s):
        out = [(1, s + 1)]
        if s == 0:
            out.append((2, 5))
        if s == 3:
            out.append((0, 0))
        return out

    table = {}
    for x in range(4):
        for y in range(4):
            for z in range(4):
                places = []
                for a, px in along(x):
                    for b, py in along(y):
                        for c, pz in along(z):
                            o = 9 * a + 3 * b + c
                            if o != 13:
                                places.append((o, px, py, pz))
                table[16 * x + 4 * y + z] = places
    return table


def iota(shape, dim):
    return lax.broadcasted_iota(jnp.int32, shape, dim)


def one_hot(cond):
    return cond.astype(F32).astype(BF16)


def dot(a, b, dims=((1,), (0,))):
    return lax.dot_general(a, b, (dims, ((), ())), preferred_element_type=F32)


def hidden_kernel(skip, coarse, child, live, face_idx, corner_idx, hidden, faces, corners):
    bricks = skip.shape[1]
    parents = coarse.shape[1] // 8
    col = iota((bricks, 8 * parents), 1)
    pick = one_hot(child[...] == (col % parents) * 8 + col // parents)
    keep = (iota((bricks, C), 0) < live[0]).astype(F32)
    for h in range(8):
        up = dot(pick, coarse[h])
        for i in range(8):
            x, y, z = 2 * (h // 4) + i // 4, 2 * (h // 2 % 2) + i // 2 % 2, 2 * (h % 2) + i % 2
            v = 16 * x + 4 * y + z
            hidden[v] = ((skip[v].astype(F32) + up) * keep).astype(BF16)
    sel = one_hot(face_idx[...] == iota((64, 2 * bricks), 1))
    for g in range(32):
        out = dot(sel, hidden[2 * g : 2 * g + 2].reshape(2 * bricks, C)).astype(BF16)
        for e in range(4):
            faces[e, g] = out[16 * e : 16 * e + 16]
    sel = one_hot(corner_idx[...] == iota((64, 8 * bricks), 1))
    for g in range(8):
        out = dot(sel, hidden[8 * g : 8 * g + 8].reshape(8 * bricks, C)).astype(BF16)
        for e in range(4):
            corners[e, g] = out[16 * e : 16 * e + 16]


def forward_kernel(hidden, faces, corners, nb, live, weight, bias, cot, act, grad, dwt, db,
                   table, pad, hot, cols):
    hot[...] = one_hot(nb[...] == iota(hot.shape, 1))
    table[:, 0:32] = hidden[...]
    for g in range(32):
        parts = [faces[e, g].astype(F32) for e in range(4)]
        for i in range(2):
            table[2 * g + i, 32:64] = jnp.concatenate(
                [p[8 * i : 8 * i + 8] for p in parts], 0).astype(BF16)
    row = iota((128, 64), 0)
    r = row % 16
    key = jnp.where(r < 8, (r // 2) * 16 + (row // 16) * 2 + r % 2, -1)
    spread = one_hot(key == iota((128, 64), 1))
    for g in range(8):
        got = jnp.concatenate([corners[e, g] for e in range(4)], 0)
        table[8 * g : 8 * g + 8, 64:80] = dot(spread, got).astype(BF16).reshape(8, 16, C)
    for x in range(4):
        pad[x + 1, 1:5, 1:5] = hidden[16 * x : 16 * x + 16].reshape(4, 4, 32, C)
    for v, places in sources().items():
        if places:
            stack = jnp.concatenate([hot[32 * o : 32 * o + 32] for o, *_ in places], 0)
            out = dot(stack, table[v]).astype(BF16)
            for i, (_, px, py, pz) in enumerate(places):
                pad[px, py, pz] = out[32 * i : 32 * i + 32]
    dwt[...] = jnp.zeros_like(dwt)
    db[...] = jnp.zeros_like(db)
    keep = (iota((512, C), 0) % 32 < live[0]).astype(F32)

    def step(x, _):
        for t in range(27):
            tx, ty, tz = t // 9, t // 3 % 3, t % 3
            cols[:, C * t : C * t + C] = pad[x + tx, ty : ty + 4, tz : tz + 4].reshape(512, C)
        pre = dot(cols[...], weight[...]) + bias[...]
        sg = 1.0 / (1.0 + jnp.exp(-pre))
        act[pl.ds(16 * x, 16)] = (pre * sg * keep).astype(BF16).reshape(16, 32, C)
        up = cot[pl.ds(16 * x, 16)].reshape(512, C).astype(F32)
        g = (up * sg * (1.0 + pre * (1.0 - sg)) * keep).astype(BF16)
        grad[pl.ds(16 * x, 16)] = g.reshape(16, 32, C)
        g32 = g.astype(F32)
        db[...] += jnp.sum(g32.reshape(64, 8, C), 0)
        dwt[...] += dot(g32.T.astype(BF16), cols[...])
        return 0

    lax.fori_loop(0, 4, step, 0)


def backward_kernel(grad, nb, weight, own, faces, corners, gp, hot, halo):
    hot[...] = one_hot(nb[...] == iota(hot.shape, 1))
    gp[...] = jnp.zeros_like(gp)

    def step(x, _):
        g = grad[pl.ds(16 * x, 16)].reshape(512, C)
        for t in range(27):
            tx, ty, tz = t // 9, t // 3 % 3, t % 3
            out = dot(g, weight[t], ((1,), (1,)))
            gp[x + tx, ty : ty + 4, tz : tz + 4] += out.reshape(4, 4, 32, C)
        return 0

    lax.fori_loop(0, 4, step, 0)
    for v, places in sources().items():
        mid = gp[v // 16 + 1, v // 4 % 4 + 1, v % 4 + 1]
        if places:
            stack = jnp.concatenate([hot[32 * o : 32 * o + 32] for o, *_ in places], 0)
            vals = jnp.concatenate([gp[a, b, c] for _, a, b, c in places], 0).astype(BF16)
            out = dot(stack, vals, ((0,), (0,)))
            own[v] = mid + out[0:32]
            halo[v] = out[32:72]
        else:
            own[v] = mid
            halo[v] = jnp.zeros((40, C), F32)
    for g in range(32):
        for e in range(4):
            faces[e, g] = halo[2 * g : 2 * g + 2, 8 * e : 8 * e + 8].reshape(16, C).astype(BF16)
    row = iota((64, 64), 0)
    key = (row % 16 // 2) * 8 + (row // 16) * 2 + row % 2
    pack = one_hot(key == iota((64, 64), 1))
    for g in range(8):
        part = halo[8 * g : 8 * g + 8, 32:40].reshape(64, C).astype(BF16)
        out = dot(pack, part).astype(BF16)
        for e in range(4):
            corners[e, g] = out[16 * e : 16 * e + 16]


def combine_kernel(own, faces, corners, child, face_idx, corner_idx, skip_grad, coarse_grad, total):
    bricks = own.shape[1]
    parents = coarse_grad.shape[1] // 8
    sel = one_hot(iota((2 * bricks, 64), 0) == face_idx[...])
    for g in range(32):
        got = jnp.concatenate([faces[e, g] for e in range(4)], 0)
        total[2 * g : 2 * g + 2] = own[2 * g : 2 * g + 2] + dot(sel, got).reshape(2, bricks, C)
    sel = one_hot(iota((8 * bricks, 64), 0) == corner_idx[...])
    for g in range(8):
        got = jnp.concatenate([corners[e, g] for e in range(4)], 0)
        new = total[8 * g : 8 * g + 8] + dot(sel, got).reshape(8, bricks, C)
        total[8 * g : 8 * g + 8] = new
        skip_grad[8 * g : 8 * g + 8] = new.astype(BF16)
    row = iota((8 * parents, bricks), 0)
    pick = one_hot((row % parents) * 8 + row // parents == child[...])
    for h in range(8):
        s = jnp.zeros((bricks, C), F32)
        for i in range(8):
            x, y, z = 2 * (h // 4) + i // 4, 2 * (h // 2 % 2) + i // 2 % 2, 2 * (h % 2) + i % 2
            s = s + total[16 * x + 4 * y + z]
        hi = s.astype(BF16)
        lo = (s - hi.astype(F32)).astype(BF16)
        coarse_grad[h] = (dot(pick, hi) + dot(pick, lo)).astype(BF16)


def call(kernel, outs, scratch, smem, *args):
    vm = pl.BlockSpec(memory_space=pltpu.VMEM)
    sm = pl.BlockSpec(memory_space=pltpu.SMEM)
    return pl.pallas_call(
        kernel,
        out_shape=[jax.ShapeDtypeStruct(s, d) for s, d in outs],
        in_specs=[sm if i in smem else vm for i in range(len(args))],
        out_specs=[vm] * len(outs),
        scratch_shapes=[pltpu.VMEM(s, d) for s, d in scratch],
        compiler_params=pltpu.CompilerParams(vmem_limit_bytes=40 * 1024 * 1024),
    )(*args)


def shift(value, step, n_x, n_y):
    route = []
    for i in range(n_x):
        for j in range(n_y):
            a, b = i + step[0], j + step[1]
            if 0 <= a < n_x and 0 <= b < n_y:
                route.append((i * n_y + j, a * n_y + b))
    return lax.ppermute(value, ("sx", "sy"), route)


def exchange(faces, corners, sign, n_x, n_y):
    moved = [
        shift(faces[k] if k < 4 else corners[k - 4], (sign * s[0], sign * s[1]), n_x, n_y)
        for k, s in enumerate(STEPS)
    ]
    return jnp.stack(moved[:4]), jnp.stack(moved[4:])


def local(n_x, n_y, skip_features, coarse_features, child_code, neighbours, send_face,
          send_corner, live_count, weight, conv_bias, cotangent):
    bricks = skip_features.shape[0]
    parents = coarse_features.shape[0]
    skip_t = skip_features.transpose(1, 0, 2)
    cot_t = cotangent.transpose(1, 0, 2)
    coarse_t = (
        coarse_features.reshape(parents, 2, 2, 2, 2, 2, 2, C)
        .transpose(2, 4, 6, 1, 3, 5, 0, 7)
        .reshape(8, 8 * parents, C)
    )
    face_idx = (send_face[0][:, None, :] + bricks * jnp.arange(2)[None, :, None]).reshape(-1)
    corner_idx = (send_corner[0][:, None, :] + bricks * jnp.arange(8)[None, :, None]).reshape(-1)
    nb = neighbours.T.reshape(-1, 1)
    pack_f, pack_c = ((4, 32, 16, C), BF16), ((4, 8, 16, C), BF16)
    hidden, faces, corners = call(
        hidden_kernel, [((64, bricks, C), BF16), pack_f, pack_c], [], (3,),
        skip_t, coarse_t, child_code[:, None], live_count, face_idx[:, None], corner_idx[:, None],
    )
    faces, corners = exchange(faces, corners, 1, n_x, n_y)
    act, grad, dwt, db = call(
        forward_kernel,
        [((64, bricks, C), BF16), ((64, bricks, C), BF16), ((C, 27 * C), F32), ((8, C), F32)],
        [((64, 80, C), BF16), ((6, 6, 6, 32, C), BF16), ((27 * 32, 80), BF16), ((512, 27 * C), BF16)],
        (4,),
        hidden, faces, corners, nb, live_count, weight.reshape(27 * C, C), conv_bias[None], cot_t,
    )
    dwt, db = lax.psum((dwt, jnp.sum(db, 0)), ("sx", "sy"))
    own, faces, corners = call(
        backward_kernel, [((64, bricks, C), F32), pack_f, pack_c],
        [((6, 6, 6, 32, C), F32), ((27 * 32, 80), BF16), ((64, 40, C), F32)], (),
        grad, nb, weight,
    )
    faces, corners = exchange(faces, corners, -1, n_x, n_y)
    skip_grad, coarse_grad = call(
        combine_kernel, [((64, bricks, C), BF16), ((8, 8 * parents, C), BF16)],
        [((64, bricks, C), F32)], (),
        own, faces, corners, child_code[None], face_idx[None], corner_idx[None],
    )
    coarse_grad = (
        coarse_grad.reshape(2, 2, 2, 2, 2, 2, parents, C)
        .transpose(6, 3, 0, 4, 1, 5, 2, 7)
        .reshape(parents, 64, C)
    )
    return (
        act.transpose(1, 0, 2),
        skip_grad.transpose(1, 0, 2),
        coarse_grad,
        dwt.reshape(C, 27, C).transpose(1, 2, 0),
        db,
    )


def solution(mesh):
    both = ("sx", "sy")
    three = P(both, None, None)
    return jax.shard_map(
        functools.partial(local, mesh.shape["sx"], mesh.shape["sy"]),
        mesh=mesh,
        in_specs=(three, three, P(both), P(both, None), three, three, P(both), P(), P(), three),
        out_specs=(three, three, three, P(), P()),
        check_vma=False,
    )
```

time: 937 us -> 202 us (0.22); the launches traced: 922 us -> 200 us
  blocking collectives: 397 us -> 39.3 us
  local copies, waits for them, and re-layouts: 253 us -> 15.3 us
  other arithmetic: 130 us -> 1.03 us
  Pallas kernels: 0 us -> 18.7 us
  matrix products: 16.4 us -> 0 us
    psum x1, blocking collectives: 397 us -> 39.3 us  [local(): dwt, db = lax.psum((dwt, jnp.sum(db, 0)), ('sx', 'sy'))]
    scatter-add x19 -> x0, local copies, waits for them, and re-layouts: 121 us -> none  [fold_taps(): grad_pad = grad_pad.at[:, tap_x:tap_x + 4, tap_y:tap_y + 4, tap_z:tap_z +...]
    scatter-add x12 -> x0, other arithmetic: 69.5 us -> none  [the longest x1 44.5 us: block_step(): table_grad.at[slot_ids.reshape(-1)].add(pieces.reshape(-1, 64, channels))]
    slice x28 -> x0, local copies, waits for them, and re-layouts: 58.2 us -> none  [the longest x2 48.2 us: fold_taps(): shaped[:, :, :, :, tap_id, :]]
    add x20 -> x2, other arithmetic: 34.8 us -> 0.82 us  [the longest x1 0.75 us: local(): send_face[0][:, None, :] + bricks * jnp.arange(2)[None, :, None]]
    gather x5 -> x0, local copies, waits for them, and re-layouts: 29 us -> none  [the longest x1 21 us: block_step(): gathered = jnp.take(brick_table, slot_ids, axis=0)]
    pallas_call x0 -> x4, Pallas kernels: none -> 18.7 us  [call(): pl.pallas_call(kernel, out_shape=[jax.ShapeDtypeStruct(s, d) for s, d in...]
    dot_general x3 -> x0, matrix products: 16.4 us -> none  [the longest x1 8.23 us: block_step(): lax.dot_general(grad_pre, flat_weight, (((1,), (1,)), ((), ())), preferre...]
  transfers between devices with their start and end apart: 17 -> 17, of which waited for: 4 -> 3; matrix products, arithmetic and copies ran while one was open for 2% -> 2% of each run, Pallas kernels for 0% -> 3%
where the time goes in v1:
time: 202 us; the launch traced here: 200 us
  waiting for transfers between devices  60.9 us (30%)
  starting transfers between devices  49.7 us (25%)
  blocking collectives  39.3 us (19%)
  Pallas kernels  18.7 us (9%)
  local copies, waits for them, and re-layouts  15.3 us (8%)
  between operations  15.2 us (8%)
    psum x1, waiting for transfers between devices, local(): dwt, db = lax.psum((dwt, jnp.sum(db, 0)), ('sx', 'sy'))  57.5 us
    ppermute x16, starting transfers between devices, shift(): return lax.ppermute(value, ('sx', 'sy'), route)  49.6 us
    psum x1, blocking collectives, local(): dwt, db = lax.psum((dwt, jnp.sum(db, 0)), ('sx', 'sy'))  39.3 us
    pallas_call x4, Pallas kernels, call(): pl.pallas_call(kernel, out_shape=[jax.ShapeDtypeStruct(s, d) for s, d in...  18.7 us
    unnamed x27, local copies, waits for them, and re-layouts  9.3 us
  transfers between devices with their start and end apart: 17, of which 3 were waited for; matrix products, arithmetic and copies ran while one was open for 2% of the time, Pallas kernels for 3%

profile of v1, /device:TPU:1, one launch (start us, length us, event | category | flops | bytes accessed | tf_op | source)
XLA Modules:
  0.0 200.1 jit_solution(7556727861299451510)
XLA Ops:
  11.4 1.4 copy.44
  13.5 5.5 %collective-permute-start.4 = (bf16[8,16,128]{2,1,0:T(8,128)(2,1)S(1)}, bf16[8,16,128]{2,1,0:T(8,128)(2,1)S(1)}, u32[]{:S(2)}, u32[]{:S(2)}) collective-permute-start(bf16[8,16,128]{2,1,0:T(8,128)(2,1)S(1)} %get-tuple-element.51), channel_id=1, source_target_pairs={{0,9},{1,10},{2,11},{3,12},{4,13},{5,14},{6,15},{8,17},{9,18},{10,... | collective-permute-start | bytes 98312 | tf_op jit(solution)/shard_map/ppermute | solution.py:204
  19.0 1.3 collective-permute-start.7
  20.3 1.9 collective-permute-start.6
  22.2 1.3 collective-permute-start.5
  23.6 5.4 %collective-permute-start = (bf16[32,16,128]{2,1,0:T(8,128)(2,1)S(1)}, bf16[32,16,128]{2,1,0:T(8,128)(2,1)S(1)}, u32[]{:S(2)}, u32[]{:S(2)}) collective-permute-start(bf16[32,16,128]{2,1,0:T(8,128)(2,1)S(1)} %get-tuple-element.43), channel_id=1, source_target_pairs={{0,8},{1,9},{2,10},{3,11},{4,12},{5,13},{6,14},{7,15},{8,16},{9,17... | collective-permute-start | bytes 393224 | tf_op jit(solution)/shard_map/ppermute | solution.py:204
  29.0 1.3 collective-permute-start.3
  30.3 5.1 %collective-permute-start.2 = (bf16[32,16,128]{2,1,0:T(8,128)(2,1)S(1)}, bf16[32,16,128]{2,1,0:T(8,128)(2,1)S(1)}, u32[]{:S(2)}, u32[]{:S(2)}) collective-permute-start(bf16[32,16,128]{2,1,0:T(8,128)(2,1)S(1)} %get-tuple-element.45), channel_id=1, source_target_pairs={{0,1},{1,2},{2,3},{3,4},{4,5},{5,6},{6,7},{8,9},{9,10},{10,11},{11... | collective-permute-start | bytes 393224 | tf_op jit(solution)/shard_map/ppermute | solution.py:204
  35.4 2.0 collective-permute-start.1
  38.4 2.3 %collective-permute-done.2 = bf16[32,16,128]{2,1,0:T(8,128)(2,1)S(1)} collective-permute-done((bf16[32,16,128]{2,1,0:T(8,128)(2,1)S(1)}, bf16[32,16,128]{2,1,0:T(8,128)(2,1)S(1)}, u32[]{:S(2)}, u32[]{:S(2)}) %collective-permute-start.2) | collective-permute-done | bytes 131104 | tf_op jit(solution)/shard_map/ppermute | solution.py:204
  41.8 11.9 %shard_map.138 = (bf16[64,32,128]{2,1,0:T(8,128)(2,1)S(1)}, bf16[64,32,128]{2,1,0:T(8,128)(2,1)S(1)}, f32[128,3456]{1,0:T(8,128)S(1)}, f32[8,128]{1,0:T(8,128)S(1)}) custom-call(bf16[64,32,128]{2,1,0:T(8,128)(2,1)S(1)} %copy-done.6, bf16[4,32,16,128]{3,2,1,0:T(8,128)(2,1)S(1)} %pad_maximum_fusion.faces, ...), custom_call_target="tpu_custom_call" | custom-call | tf_op jit(solution)/shard_map/pallas_call | solution.py:187
  55.3 1.7 copy.38
  58.0 5.6 %shard_map.139 = (f32[64,32,128]{2,1,0:T(8,128)S(1)}, bf16[4,32,16,128]{3,2,1,0:T(8,128)(2,1)S(1)}, bf16[4,8,16,128]{3,2,1,0:T(8,128)(2,1)S(1)}) custom-call(bf16[64,32,128]{2,1,0:T(8,128)(2,1)S(1)} %copy-done.2, s32[864,1]{1,0:T(8,128)S(1)} %reshape.138.nb, bf16[27,128,128]{2,1,0:T(8,128)(2,1)S(1)} %copy-done), custom_call_target="tpu_custom_call" | custom-call | tf_op jit(solution)/shard_map/pallas_call | solution.py:187
  63.6 1.3 collective-permute-start.12
  64.9 5.2 %collective-permute-start.15 = (bf16[8,16,128]{2,1,0:T(8,128)(2,1)S(1)}, bf16[8,16,128]{2,1,0:T(8,128)(2,1)S(1)}, u32[]{:S(2)}, u32[]{:S(2)}) collective-permute-start(bf16[8,16,128]{2,1,0:T(8,128)(2,1)S(1)} %get-tuple-element.48), channel_id=1, source_target_pairs={{0,9},{1,10},{2,11},{3,12},{4,13},{5,14},{6,15},{8,17},{9,18},{10,... | collective-permute-start | bytes 98312 | tf_op jit(solution)/shard_map/ppermute | solution.py:204
  70.1 1.3 collective-permute-start.14
  71.4 4.3 %collective-permute-start.13 = (bf16[8,16,128]{2,1,0:T(8,128)(2,1)S(1)}, bf16[8,16,128]{2,1,0:T(8,128)(2,1)S(1)}, u32[]{:S(2)}, u32[]{:S(2)}) collective-permute-start(bf16[8,16,128]{2,1,0:T(8,128)(2,1)S(1)} %get-tuple-element.50), channel_id=1, source_target_pairs={{8,1},{9,2},{10,3},{11,4},{12,5},{13,6},{14,7},{16,9},{17,10},{18,... | collective-permute-start | bytes 98312 | tf_op jit(solution)/shard_map/ppermute | solution.py:204
  75.7 1.9 collective-permute-start.8
  77.7 6.8 %collective-permute-start.11 = (bf16[32,16,128]{2,1,0:T(8,128)(2,1)S(1)}, bf16[32,16,128]{2,1,0:T(8,128)(2,1)S(1)}, u32[]{:S(2)}, u32[]{:S(2)}) collective-permute-start(bf16[32,16,128]{2,1,0:T(8,128)(2,1)S(1)} %get-tuple-element.40), channel_id=1, source_target_pairs={{0,1},{1,2},{2,3},{3,4},{4,5},{5,6},{6,7},{8,9},{9,10},{10,11},{11... | collective-permute-start | bytes 393224 | tf_op jit(solution)/shard_map/ppermute | solution.py:204
  84.4 1.3 collective-permute-start.10
  85.8 3.9 %collective-permute-start.9 = (bf16[32,16,128]{2,1,0:T(8,128)(2,1)S(1)}, bf16[32,16,128]{2,1,0:T(8,128)(2,1)S(1)}, u32[]{:S(2)}, u32[]{:S(2)}) collective-permute-start(bf16[32,16,128]{2,1,0:T(8,128)(2,1)S(1)} %get-tuple-element.42), channel_id=1, source_target_pairs={{0,8},{1,9},{2,10},{3,11},{4,12},{5,13},{6,14},{7,15},{8,16},{9,17... | collective-permute-start | bytes 393224 | tf_op jit(solution)/shard_map/ppermute | solution.py:204
  90.9 39.3 %psum.15 = f32[128]{0:T(128)} all-reduce(f32[128]{0:T(128)S(1)} %reduce_sum.9), channel_id=1, replica_groups=mesh['sx'=4,'sy'=8] {'sx','sy'}, use_global_device_ids=true, to_apply=%region_2.0 | all-reduce | flops 128 | bytes 1024 | tf_op jit(solution)/shard_map/psum | solution.py:242
  132.8 57.5 %all-reduce.2.cloned.1.call-done = f32[27,128,128]{2,1,0:T(8,128)} async-done(((f32[27,128,128]{2,1,0:T(8,128)}), f32[27,128,128]{2,1,0:T(8,128)}) %all-reduce.2.cloned.1.call-update) | async-done | bytes 1769488 | tf_op jit(solution)/shard_map/psum | solution.py:242
  190.3 2.9 %copy.47 = f32[27,128,128]{2,1,0:T(8,128)} copy(f32[27,128,128]{2,1,0:T(8,128)} %all-reduce.2.cloned.1.call-done) | data formatting | bytes 3538944
  (67 shorter events, 12.7 us)
Async XLA Ops:
  7.2 30.2 %copy-start.10 = (s32[32,27]{1,0:T(8,128)S(1)}, s32[32,27]{1,0:T(8,128)}, u32[]{:S(2)}) copy-start(s32[32,27]{1,0:T(8,128)} %param.13) | copy-start | bytes 10372
  7.2 183.2 %all-reduce.2.cloned.1.call-start = ((), (), s32[]{:S(2)}) async-start(), calls=%async_computation | async-start | bytes 3538944 | tf_op jit(solution)/shard_map/psum | solution.py:242
  11.4 26.6 %copy-start.9 = (bf16[32,64,128]{2,1,0:T(8,128)(2,1)S(1)}, bf16[32,64,128]{2,1,0:T(8,128)(2,1)}, u32[]{:S(2)}) copy-start(bf16[32,64,128]{2,1,0:T(8,128)(2,1)} %param.19) | copy-start | bytes 1572868
  13.5 10.1 %copy-start.5 = (bf16[64,32,128]{2,1,0:T(8,128)(2,1)}, bf16[64,32,128]{2,1,0:T(8,128)(2,1)S(1)}, u32[]{:S(2)}) copy-start(bf16[64,32,128]{2,1,0:T(8,128)(2,1)S(1)} %get-tuple-element.17.hidden) | copy-start | bytes 1572868
  13.5 15.5 %collective-permute-start.4 = (bf16[8,16,128]{2,1,0:T(8,128)(2,1)S(1)}, bf16[8,16,128]{2,1,0:T(8,128)(2,1)S(1)}, u32[]{:S(2)}, u32[]{:S(2)}) collective-permute-start(bf16[8,16,128]{2,1,0:T(8,128)(2,1)S(1)} %get-tuple-element.51), channel_id=1, source_target_pairs={{0,9},{1,10},{2,11},{3,12},{4,13},{5,14},{6,15},{8,17},{9,18},{10,... | collective-permute-start | bytes 98312 | tf_op jit(solution)/shard_map/ppermute | solution.py:204
  19.0 11.3 %collective-permute-start.7 = (bf16[8,16,128]{2,1,0:T(8,128)(2,1)S(1)}, bf16[8,16,128]{2,1,0:T(8,128)(2,1)S(1)}, u32[]{:S(2)}, u32[]{:S(2)}) collective-permute-start(bf16[8,16,128]{2,1,0:T(8,128)(2,1)S(1)} %get-tuple-element.52), channel_id=1, source_target_pairs={{9,0},{10,1},{11,2},{12,3},{13,4},{14,5},{15,6},{17,8},{18,9},{19,... | collective-permute-start | bytes 98312 | tf_op jit(solution)/shard_map/ppermute | solution.py:204
  20.3 15.1 %collective-permute-start.6 = (bf16[8,16,128]{2,1,0:T(8,128)(2,1)S(1)}, bf16[8,16,128]{2,1,0:T(8,128)(2,1)S(1)}, u32[]{:S(2)}, u32[]{:S(2)}) collective-permute-start(bf16[8,16,128]{2,1,0:T(8,128)(2,1)S(1)} %get-tuple-element.53), channel_id=1, source_target_pairs={{8,1},{9,2},{10,3},{11,4},{12,5},{13,6},{14,7},{16,9},{17,10},{18,... | collective-permute-start | bytes 98312 | tf_op jit(solution)/shard_map/ppermute | solution.py:204
  22.2 16.1 %collective-permute-start.5 = (bf16[8,16,128]{2,1,0:T(8,128)(2,1)S(1)}, bf16[8,16,128]{2,1,0:T(8,128)(2,1)S(1)}, u32[]{:S(2)}, u32[]{:S(2)}) collective-permute-start(bf16[8,16,128]{2,1,0:T(8,128)(2,1)S(1)} %get-tuple-element.54), channel_id=1, source_target_pairs={{1,8},{2,9},{3,10},{4,11},{5,12},{6,13},{7,14},{9,16},{10,17},{11,... | collective-permute-start | bytes 98312 | tf_op jit(solution)/shard_map/ppermute | solution.py:204
  23.5 18.2 %copy-start = (bf16[27,128,128]{2,1,0:T(8,128)(2,1)S(1)}, bf16[27,128,128]{2,1,0:T(8,128)(2,1)}, u32[]{:S(2)}) copy-start(bf16[27,128,128]{2,1,0:T(8,128)(2,1)} %weight.1) | copy-start | bytes 2654212
  23.5 18.2 %copy-start.8 = (f32[128]{0:T(128)S(1)}, f32[128]{0:T(128)}, u32[]{:S(2)}) copy-start(f32[128]{0:T(128)} %param.18) | copy-start | bytes 1540
  23.6 14.7 %collective-permute-start = (bf16[32,16,128]{2,1,0:T(8,128)(2,1)S(1)}, bf16[32,16,128]{2,1,0:T(8,128)(2,1)S(1)}, u32[]{:S(2)}, u32[]{:S(2)}) collective-permute-start(bf16[32,16,128]{2,1,0:T(8,128)(2,1)S(1)} %get-tuple-element.43), channel_id=1, source_target_pairs={{0,8},{1,9},{2,10},{3,11},{4,12},{5,13},{6,14},{7,15},{8,16},{9,17... | collective-permute-start | bytes 393224 | tf_op jit(solution)/shard_map/ppermute | solution.py:204
  29.0 9.4 %collective-permute-start.3 = (bf16[32,16,128]{2,1,0:T(8,128)(2,1)S(1)}, bf16[32,16,128]{2,1,0:T(8,128)(2,1)S(1)}, u32[]{:S(2)}, u32[]{:S(2)}) collective-permute-start(bf16[32,16,128]{2,1,0:T(8,128)(2,1)S(1)} %get-tuple-element.44), channel_id=1, source_target_pairs={{1,0},{2,1},{3,2},{4,3},{5,4},{6,5},{7,6},{9,8},{10,9},{11,10},{12... | collective-permute-start | bytes 393224 | tf_op jit(solution)/shard_map/ppermute | solution.py:204
  30.3 10.4 %collective-permute-start.2 = (bf16[32,16,128]{2,1,0:T(8,128)(2,1)S(1)}, bf16[32,16,128]{2,1,0:T(8,128)(2,1)S(1)}, u32[]{:S(2)}, u32[]{:S(2)}) collective-permute-start(bf16[32,16,128]{2,1,0:T(8,128)(2,1)S(1)} %get-tuple-element.45), channel_id=1, source_target_pairs={{0,1},{1,2},{2,3},{3,4},{4,5},{5,6},{6,7},{8,9},{9,10},{10,11},{11... | collective-permute-start | bytes 393224 | tf_op jit(solution)/shard_map/ppermute | solution.py:204
  35.4 6.3 %collective-permute-start.1 = (bf16[32,16,128]{2,1,0:T(8,128)(2,1)S(1)}, bf16[32,16,128]{2,1,0:T(8,128)(2,1)S(1)}, u32[]{:S(2)}, u32[]{:S(2)}) collective-permute-start(bf16[32,16,128]{2,1,0:T(8,128)(2,1)S(1)} %get-tuple-element.46), channel_id=1, source_target_pairs={{8,0},{9,1},{10,2},{11,3},{12,4},{13,5},{14,6},{15,7},{16,8},{17,9... | collective-permute-start | bytes 393224 | tf_op jit(solution)/shard_map/ppermute | solution.py:204
  57.0 32.9 %copy-start.4 = (bf16[64,32,128]{2,1,0:T(8,128)(2,1)S(1)}, bf16[64,32,128]{2,1,0:T(8,128)(2,1)}, u32[]{:S(2)}) copy-start(bf16[64,32,128]{2,1,0:T(8,128)(2,1)} %copy-done.3) | copy-start | bytes 1572868
  63.6 66.8 %copy-start.7 = (s32[32]{0:T(128)S(1)}, s32[32]{0:T(128)}, u32[]{:S(2)}) copy-start(s32[32]{0:T(128)} %param.12) | copy-start | bytes 388
  63.6 14.0 %collective-permute-start.12 = (bf16[8,16,128]{2,1,0:T(8,128)(2,1)S(1)}, bf16[8,16,128]{2,1,0:T(8,128)(2,1)S(1)}, u32[]{:S(2)}, u32[]{:S(2)}) collective-permute-start(bf16[8,16,128]{2,1,0:T(8,128)(2,1)S(1)} %get-tuple-element.47), channel_id=1, source_target_pairs={{9,0},{10,1},{11,2},{12,3},{13,4},{14,5},{15,6},{17,8},{18,9},{19,... | collective-permute-start | bytes 98312 | tf_op jit(solution)/shard_map/ppermute | solution.py:204
  64.9 19.5 %collective-permute-start.15 = (bf16[8,16,128]{2,1,0:T(8,128)(2,1)S(1)}, bf16[8,16,128]{2,1,0:T(8,128)(2,1)S(1)}, u32[]{:S(2)}, u32[]{:S(2)}) collective-permute-start(bf16[8,16,128]{2,1,0:T(8,128)(2,1)S(1)} %get-tuple-element.48), channel_id=1, source_target_pairs={{0,9},{1,10},{2,11},{3,12},{4,13},{5,14},{6,15},{8,17},{9,18},{10,... | collective-permute-start | bytes 98312 | tf_op jit(solution)/shard_map/ppermute | solution.py:204
  70.1 15.6 %collective-permute-start.14 = (bf16[8,16,128]{2,1,0:T(8,128)(2,1)S(1)}, bf16[8,16,128]{2,1,0:T(8,128)(2,1)S(1)}, u32[]{:S(2)}, u32[]{:S(2)}) collective-permute-start(bf16[8,16,128]{2,1,0:T(8,128)(2,1)S(1)} %get-tuple-element.49), channel_id=1, source_target_pairs={{1,8},{2,9},{3,10},{4,11},{5,12},{6,13},{7,14},{9,16},{10,17},{11,... | collective-permute-start | bytes 98312 | tf_op jit(solution)/shard_map/ppermute | solution.py:204
  71.4 58.8 %collective-permute-start.13 = (bf16[8,16,128]{2,1,0:T(8,128)(2,1)S(1)}, bf16[8,16,128]{2,1,0:T(8,128)(2,1)S(1)}, u32[]{:S(2)}, u32[]{:S(2)}) collective-permute-start(bf16[8,16,128]{2,1,0:T(8,128)(2,1)S(1)} %get-tuple-element.50), channel_id=1, source_target_pairs={{8,1},{9,2},{10,3},{11,4},{12,5},{13,6},{14,7},{16,9},{17,10},{18,... | collective-permute-start | bytes 98312 | tf_op jit(solution)/shard_map/ppermute | solution.py:204
  75.7 54.5 %collective-permute-start.8 = (bf16[32,16,128]{2,1,0:T(8,128)(2,1)S(1)}, bf16[32,16,128]{2,1,0:T(8,128)(2,1)S(1)}, u32[]{:S(2)}, u32[]{:S(2)}) collective-permute-start(bf16[32,16,128]{2,1,0:T(8,128)(2,1)S(1)} %get-tuple-element.39), channel_id=1, source_target_pairs={{8,0},{9,1},{10,2},{11,3},{12,4},{13,5},{14,6},{15,7},{16,8},{17,9... | collective-permute-start | bytes 393224 | tf_op jit(solution)/shard_map/ppermute | solution.py:204
  77.7 52.6 %collective-permute-start.11 = (bf16[32,16,128]{2,1,0:T(8,128)(2,1)S(1)}, bf16[32,16,128]{2,1,0:T(8,128)(2,1)S(1)}, u32[]{:S(2)}, u32[]{:S(2)}) collective-permute-start(bf16[32,16,128]{2,1,0:T(8,128)(2,1)S(1)} %get-tuple-element.40), channel_id=1, source_target_pairs={{0,1},{1,2},{2,3},{3,4},{4,5},{5,6},{6,7},{8,9},{9,10},{10,11},{11... | collective-permute-start | bytes 393224 | tf_op jit(solution)/shard_map/ppermute | solution.py:204
  84.4 45.8 %collective-permute-start.10 = (bf16[32,16,128]{2,1,0:T(8,128)(2,1)S(1)}, bf16[32,16,128]{2,1,0:T(8,128)(2,1)S(1)}, u32[]{:S(2)}, u32[]{:S(2)}) collective-permute-start(bf16[32,16,128]{2,1,0:T(8,128)(2,1)S(1)} %get-tuple-element.41), channel_id=1, source_target_pairs={{1,0},{2,1},{3,2},{4,3},{5,4},{6,5},{7,6},{9,8},{10,9},{11,10},{12... | collective-permute-start | bytes 393224 | tf_op jit(solution)/shard_map/ppermute | solution.py:204
  85.8 44.5 %collective-permute-start.9 = (bf16[32,16,128]{2,1,0:T(8,128)(2,1)S(1)}, bf16[32,16,128]{2,1,0:T(8,128)(2,1)S(1)}, u32[]{:S(2)}, u32[]{:S(2)}) collective-permute-start(bf16[32,16,128]{2,1,0:T(8,128)(2,1)S(1)} %get-tuple-element.42), channel_id=1, source_target_pairs={{0,8},{1,9},{2,10},{3,11},{4,12},{5,13},{6,14},{7,15},{8,16},{9,17... | collective-permute-start | bytes 393224 | tf_op jit(solution)/shard_map/ppermute | solution.py:204
  (4 other events, 6.5 us)
Sparse Core Ops, SparseCore 0:
  57.1 133.1 all-reduce.1

commit v2 on v1

--- a/solution.py
+++ b/solution.py
@@ -9,6 +9,7 @@
 
 F32 = jnp.float32
 BF16 = jnp.bfloat16
+MESH = pl.DeviceIdType.MESH
 C = 128
 STEPS = ((1, 0), (-1, 0), (0, 1), (0, -1), (1, 1), (1, -1), (-1, 1), (-1, -1))
 
@@ -49,7 +50,64 @@
     return lax.dot_general(a, b, (dims, ((), ())), preferred_element_type=F32)
 
 
-def hidden_kernel(skip, coarse, child, live, face_idx, corner_idx, hidden, faces, corners):
+def partners(sign, n_x, n_y):
+    i, j = lax.axis_index("sx"), lax.axis_index("sy")
+
+    def inside(a, b):
+        return (a >= 0) & (a < n_x) & (b >= 0) & (b < n_y)
+
+    return [
+        (
+            inside(i + sign * a, j + sign * b),
+            inside(i - sign * a, j - sign * b),
+            (jnp.clip(i + sign * a, 0, n_x - 1), jnp.clip(j + sign * b, 0, n_y - 1)),
+        )
+        for a, b in STEPS
+    ]
+
+
+def greet(sign, n_x, n_y):
+    barrier = pltpu.get_barrier_semaphore()
+    places = partners(sign, n_x, n_y)
+    for out, _, target in places:
+        @pl.when(out)
+        def _():
+            pl.semaphore_signal(barrier, inc=1, device_id=target, device_id_type=MESH)
+    pl.semaphore_wait(barrier, sum(out.astype(jnp.int32) for out, _, _ in places))
+
+
+def exchange(faces, corners, got_faces, got_corners, send_sem, recv_sem, sign, n_x, n_y):
+    places = partners(sign, n_x, n_y)
+
+    def copy(k):
+        src, dst = (faces, got_faces) if k < 4 else (corners, got_corners)
+        return pltpu.make_async_remote_copy(
+            src_ref=src.at[k % 4], dst_ref=dst.at[k % 4], send_sem=send_sem.at[k],
+            recv_sem=recv_sem.at[k], device_id=places[k][2], device_id_type=MESH)
+
+    for k in range(8):
+        @pl.when(places[k][0])
+        def _():
+            copy(k).start()
+    for k in range(8):
+        dst = got_faces if k < 4 else got_corners
+
+        @pl.when(jnp.logical_not(places[k][1]))
+        def _():
+            dst[k % 4] = jnp.zeros_like(dst[k % 4])
+    for k in range(8):
+        @pl.when(places[k][1])
+        def _():
+            copy(k).wait_recv()
+    for k in range(8):
+        @pl.when(places[k][0])
+        def _():
+            copy(k).wait_send()
+
+
+def hidden_kernel(n_x, n_y, skip, coarse, child, live, face_idx, corner_idx, hidden, got_faces,
+                  got_corners, faces, corners, send_sem, recv_sem):
+    greet(1, n_x, n_y)
     bricks = skip.shape[1]
     parents = coarse.shape[1] // 8
     col = iota((bricks, 8 * parents), 1)
@@ -71,9 +129,10 @@
         out = dot(sel, hidden[8 * g : 8 * g + 8].reshape(8 * bricks, C)).astype(BF16)
         for e in range(4):
             corners[e, g] = out[16 * e : 16 * e + 16]
-
-
-def forward_kernel(hidden, faces, corners, nb, live, weight, bias, cot, act, grad, dwt, db,
+    exchange(faces, corners, got_faces, got_corners, send_sem, recv_sem, 1, n_x, n_y)
+
+
+def forward_kernel(hidden, faces, corners, nb, live, weight, bias, cot, act, grad, dwt,
                    table, pad, hot, cols):
     hot[...] = one_hot(nb[...] == iota(hot.shape, 1))
     table[:, 0:32] = hidden[...]
@@ -98,22 +157,20 @@
             for i, (_, px, py, pz) in enumerate(places):
                 pad[px, py, pz] = out[32 * i : 32 * i + 32]
     dwt[...] = jnp.zeros_like(dwt)
-    db[...] = jnp.zeros_like(db)
+    cols[:, 27 * C :] = jnp.ones((512, C), BF16)
     keep = (iota((512, C), 0) % 32 < live[0]).astype(F32)
 
     def step(x, _):
         for t in range(27):
             tx, ty, tz = t // 9, t // 3 % 3, t % 3
             cols[:, C * t : C * t + C] = pad[x + tx, ty : ty + 4, tz : tz + 4].reshape(512, C)
-        pre = dot(cols[...], weight[...]) + bias[...]
+        pre = dot(cols[:, : 27 * C], weight[...]) + bias[...]
         sg = 1.0 / (1.0 + jnp.exp(-pre))
         act[pl.ds(16 * x, 16)] = (pre * sg * keep).astype(BF16).reshape(16, 32, C)
         up = cot[pl.ds(16 * x, 16)].reshape(512, C).astype(F32)
         g = (up * sg * (1.0 + pre * (1.0 - sg)) * keep).astype(BF16)
         grad[pl.ds(16 * x, 16)] = g.reshape(16, 32, C)
-        g32 = g.astype(F32)
-        db[...] += jnp.sum(g32.reshape(64, 8, C), 0)
-        dwt[...] += dot(g32.T.astype(BF16), cols[...])
+        dwt[...] += dot(g.astype(F32).T.astype(BF16), cols[...])
         return 0
 
     lax.fori_loop(0, 4, step, 0)
@@ -156,7 +213,10 @@
             corners[e, g] = out[16 * e : 16 * e + 16]
 
 
-def combine_kernel(own, faces, corners, child, face_idx, corner_idx, skip_grad, coarse_grad, total):
+def combine_kernel(n_x, n_y, own, sent_faces, sent_corners, child, face_idx, corner_idx, skip_grad,
+                   coarse_grad, total, faces, corners, send_sem, recv_sem):
+    greet(-1, n_x, n_y)
+    exchange(sent_faces, sent_corners, faces, corners, send_sem, recv_sem, -1, n_x, n_y)
     bricks = own.shape[1]
     parents = coarse_grad.shape[1] // 8
     sel = one_hot(iota((2 * bricks, 64), 0) == face_idx[...])
@@ -181,35 +241,22 @@
         coarse_grad[h] = (dot(pick, hi) + dot(pick, lo)).astype(BF16)
 
 
-def call(kernel, outs, scratch, smem, *args):
+def call(kernel, outs, scratch, smem, *args, collective=None):
     vm = pl.BlockSpec(memory_space=pltpu.VMEM)
     sm = pl.BlockSpec(memory_space=pltpu.SMEM)
+    sems = [] if collective is None else [pltpu.SemaphoreType.DMA((8,))] * 2
     return pl.pallas_call(
         kernel,
         out_shape=[jax.ShapeDtypeStruct(s, d) for s, d in outs],
         in_specs=[sm if i in smem else vm for i in range(len(args))],
         out_specs=[vm] * len(outs),
-        scratch_shapes=[pltpu.VMEM(s, d) for s, d in scratch],
-        compiler_params=pltpu.CompilerParams(vmem_limit_bytes=40 * 1024 * 1024),
+        scratch_shapes=[pltpu.VMEM(s, d) for s, d in scratch] + sems,
+        compiler_params=pltpu.CompilerParams(
+            vmem_limit_bytes=40 * 1024 * 1024,
+            collective_id=collective,
+            has_side_effects=collective is not None,
+        ),
     )(*args)
-
-
-def shift(value, step, n_x, n_y):
-    route = []
-    for i in range(n_x):
-        for j in range(n_y):
-            a, b = i + step[0], j + step[1]
-            if 0 <= a < n_x and 0 <= b < n_y:
-                route.append((i * n_y + j, a * n_y + b))
-    return lax.ppermute(value, ("sx", "sy"), route)
-
-
-def exchange(faces, corners, sign, n_x, n_y):
-    moved = [
-        shift(faces[k] if k < 4 else corners[k - 4], (sign * s[0], sign * s[1]), n_x, n_y)
-        for k, s in enumerate(STEPS)
-    ]
-    return jnp.stack(moved[:4]), jnp.stack(moved[4:])
 
 
 def local(n_x, n_y, skip_features, coarse_features, child_code, neighbours, send_face,
@@ -228,28 +275,30 @@
     nb = neighbours.T.reshape(-1, 1)
     pack_f, pack_c = ((4, 32, 16, C), BF16), ((4, 8, 16, C), BF16)
     hidden, faces, corners = call(
-        hidden_kernel, [((64, bricks, C), BF16), pack_f, pack_c], [], (3,),
+        functools.partial(hidden_kernel, n_x, n_y),
+        [((64, bricks, C), BF16), pack_f, pack_c], [pack_f, pack_c], (3,),
         skip_t, coarse_t, child_code[:, None], live_count, face_idx[:, None], corner_idx[:, None],
-    )
-    faces, corners = exchange(faces, corners, 1, n_x, n_y)
-    act, grad, dwt, db = call(
+        collective=0,
+    )
+    act, grad, dwt = call(
         forward_kernel,
-        [((64, bricks, C), BF16), ((64, bricks, C), BF16), ((C, 27 * C), F32), ((8, C), F32)],
-        [((64, 80, C), BF16), ((6, 6, 6, 32, C), BF16), ((27 * 32, 80), BF16), ((512, 27 * C), BF16)],
+        [((64, bricks, C), BF16), ((64, bricks, C), BF16), ((C, 28 * C), F32)],
+        [((64, 80, C), BF16), ((6, 6, 6, 32, C), BF16), ((27 * 32, 80), BF16), ((512, 28 * C), BF16)],
         (4,),
         hidden, faces, corners, nb, live_count, weight.reshape(27 * C, C), conv_bias[None], cot_t,
     )
-    dwt, db = lax.psum((dwt, jnp.sum(db, 0)), ("sx", "sy"))
+    dwt = lax.psum(dwt, ("sx", "sy"))
     own, faces, corners = call(
         backward_kernel, [((64, bricks, C), F32), pack_f, pack_c],
         [((6, 6, 6, 32, C), F32), ((27 * 32, 80), BF16), ((64, 40, C), F32)], (),
         grad, nb, weight,
     )
-    faces, corners = exchange(faces, corners, -1, n_x, n_y)
     skip_grad, coarse_grad = call(
-        combine_kernel, [((64, bricks, C), BF16), ((8, 8 * parents, C), BF16)],
-        [((64, bricks, C), F32)], (),
+        functools.partial(combine_kernel, n_x, n_y),
+        [((64, bricks, C), BF16), ((8, 8 * parents, C), BF16)],
+        [((64, bricks, C), F32), pack_f, pack_c], (),
         own, faces, corners, child_code[None], face_idx[None], corner_idx[None],
+        collective=1,
     )
     coarse_grad = (
         coarse_grad.reshape(2, 2, 2, 2, 2, 2, parents, C)
@@ -260,8 +309,8 @@
         act.transpose(1, 0, 2),
         skip_grad.transpose(1, 0, 2),
         coarse_grad,
-        dwt.reshape(C, 27, C).transpose(1, 2, 0),
-        db,
+        dwt[:, : 27 * C].reshape(C, 27, C).transpose(1, 2, 0),
+        dwt[:, 27 * C],
     )
 
 

time: 202 us -> 187 us (0.926)
  starting transfers between devices: 49.7 us -> 0.04 us
  waiting for transfers between devices: 60.9 us -> 110 us
  blocking collectives: 39.3 us -> 0 us
  Pallas kernels: 18.7 us -> 45.2 us
    psum x1, waiting for transfers between devices: 57.5 us -> 110 us  [local(): dwt = lax.psum(dwt, ('sx', 'sy'))]
    ppermute x16 -> x0, starting transfers between devices: 49.6 us -> none  [shift(): return lax.ppermute(value, ('sx', 'sy'), route)]
    psum x1 -> x0, blocking collectives: 39.3 us -> none  [local(): dwt, db = lax.psum((dwt, jnp.sum(db, 0)), ('sx', 'sy'))]
    pallas_call x4, Pallas kernels: 18.7 us -> 45.2 us  [call(): pl.pallas_call(kernel, out_shape=[jax.ShapeDtypeStruct(s, d) for s, d in...]
    unnamed x27 -> x12, local copies, waits for them, and re-layouts: 9.3 us -> 3.75 us
    slice x0 -> x4, local copies, waits for them, and re-layouts: none -> 4.63 us  [the longest x3 3.16 us: local(): dwt[:, :27 * C].reshape(C, 27, C).transpose(1, 2, 0)]
    ppermute x16 -> x0, waiting for transfers between devices: 3.36 us -> none  [shift(): return lax.ppermute(value, ('sx', 'sy'), route)]
  transfers between devices with their start and end apart: 17 -> 1, of which waited for: 3 -> 1; matrix products, arithmetic and copies ran while one was open for 2% -> 2% of each run, Pallas kernels for 3% -> 11%
where the time goes in v2:
time: 187 us; the launch traced here: 185 us
  waiting for transfers between devices  110 us (59%)
  Pallas kernels  45.2 us (24%)
  between operations  14.8 us (8%)
  local copies, waits for them, and re-layouts  13.3 us (7%)
    psum x1, waiting for transfers between devices, local(): dwt = lax.psum(dwt, ('sx', 'sy'))  110 us
    pallas_call x4, Pallas kernels, call(): pl.pallas_call(kernel, out_shape=[jax.ShapeDtypeStruct(s, d) for s, d in...  45.2 us
    unnamed x12, local copies, waits for them, and re-layouts  3.75 us
  transfers between devices with their start and end apart: 1, of which 1 were waited for; matrix products, arithmetic and copies ran while one was open for 2% of the time, Pallas kernels for 11%

profile of v2, /device:TPU:1, one launch (start us, length us, event | category | flops | bytes accessed | tf_op | source)
XLA Modules:
  0.0 184.6 jit_solution(158522935339491392)
XLA Ops:
  7.9 0.8 copy.29
  8.7 0.1 broadcast_add_fusion
  8.8 0.1 add.85.corner_idx
  8.9 0.9 copy.33
  9.7 0.7 copy.30.child
  10.5 0.8 broadcast_add_fusion.1
  11.2 0.1 add.84.face_idx
  11.3 1.0 copy.28
  12.3 0.5 reshape.138.nb
  12.8 1.4 copy.44
  14.2 0.3 copy.43
  14.5 12.3 %shard_map.137 = (bf16[64,32,128]{2,1,0:T(8,128)(2,1)S(1)}, bf16[4,32,16,128]{3,2,1,0:T(8,128)(2,1)S(1)}, bf16[4,8,16,128]{3,2,1,0:T(8,128)(2,1)S(1)}) custom-call(bf16[64,32,128]{2,1,0:T(8,128)(2,1)S(1)} %bitcast.27, bf16[8,64,128]{2,1,0:T(8,128)(2,1)S(1)} %bitcast.29, s32[32,1]{1,0:T(8,128)S(1)} %copy.30.child, s32[1]{0:T(128)S(6)} %copy.46.live, ...), custom_call_target="tpu_custom_call" | custom-call | tf_op jit(solution)/shard_map/pallas_call | solution.py:248
  26.8 13.2 %shard_map.138 = (bf16[64,32,128]{2,1,0:T(8,128)(2,1)S(1)}, bf16[64,32,128]{2,1,0:T(8,128)(2,1)S(1)}, f32[128,3584]{1,0:T(8,128)}) custom-call(bf16[64,32,128]{2,1,0:T(8,128)(2,1)S(1)} %get-tuple-element.16.hidden, bf16[4,32,16,128]{3,2,1,0:T(8,128)(2,1)S(1)} %get-tuple-element.17.faces, bf16[4,8,16,128]{3,2,1,0:T(8,128)(2,1)S(1)} %get-tuple-element.18.corners, ...), custom_call_target="tpu_custom_call" | custom-call | tf_op jit(solution)/shard_map/pallas_call | solution.py:248
  40.0 0.1 add.82.face_idx
  40.1 0.1 add.83.corner_idx
  40.2 1.0 copy.39
  41.2 5.6 %shard_map.139 = (f32[64,32,128]{2,1,0:T(8,128)S(1)}, bf16[4,32,16,128]{3,2,1,0:T(8,128)(2,1)S(1)}, bf16[4,8,16,128]{3,2,1,0:T(8,128)(2,1)S(1)}) custom-call(bf16[64,32,128]{2,1,0:T(8,128)(2,1)S(1)} %get-tuple-element.20.grad, s32[864,1]{1,0:T(8,128)S(1)} %reshape.138.nb, bf16[27,128,128]{2,1,0:T(8,128)(2,1)S(1)} %copy-done), custom_call_target="tpu_custom_call" | custom-call | tf_op jit(solution)/shard_map/pallas_call | solution.py:248
  46.9 14.2 %shard_map.140 = (bf16[64,32,128]{2,1,0:T(8,128)(2,1)S(1)}, bf16[8,64,128]{2,1,0:T(8,128)(2,1)S(1)}) custom-call(f32[64,32,128]{2,1,0:T(8,128)S(1)} %get-tuple-element.21.own, bf16[4,32,16,128]{3,2,1,0:T(8,128)(2,1)S(1)} %get-tuple-element.22.sent_faces, bf16[4,8,16,128]{3,2,1,0:T(8,128)(2,1)S(1)} %get-tuple-element.23.sent_corners, s32[1,32]{1,0:T(1,128)S(1)} %bitcast.34, ...), custom_call_target="tpu_custom_call" | custom-call | tf_op jit(solution)/shard_map/pallas_call | solution.py:248
  61.0 1.0 copy.40
  62.0 0.8 copy.37
  62.8 110.3 %all-reduce.2.cloned.1.call-done = f32[128,3584]{1,0:T(8,128)} async-done(((f32[128,3584]{1,0:T(8,128)}), f32[128,3584]{1,0:T(8,128)}) %all-reduce.2.cloned.1.call-update) | async-done | bytes 1835024 | tf_op jit(solution)/shard_map/psum | solution.py:290
  173.2 1.5 slice-done
  174.6 1.7 copy.38
  176.3 1.5 slice_reduce_fusion
  (13 shorter events, 0.1 us)
Async XLA Ops:
  7.2 7.0 %copy-start.3 = (bf16[32,64,128]{2,1,0:T(8,128)(2,1)S(1)}, bf16[32,64,128]{2,1,0:T(8,128)(2,1)}, u32[]{:S(2)}) copy-start(bf16[32,64,128]{2,1,0:T(8,128)(2,1)} %param.19) | copy-start | bytes 1572868
  7.2 166.0 %all-reduce.2.cloned.1.call-start = ((), (), s32[]{:S(2)}) async-start(), calls=%async_computation | async-start | bytes 3670016 | tf_op jit(solution)/shard_map/psum | solution.py:290
  8.9 17.9 %copy-start = (bf16[27,128,128]{2,1,0:T(8,128)(2,1)S(1)}, bf16[27,128,128]{2,1,0:T(8,128)(2,1)}, u32[]{:S(2)}) copy-start(bf16[27,128,128]{2,1,0:T(8,128)(2,1)} %weight.1) | copy-start | bytes 2654212
  8.9 18.0 %copy-start.2 = (f32[128]{0:T(128)S(1)}, f32[128]{0:T(128)}, u32[]{:S(2)}) copy-start(f32[128]{0:T(128)} %param.18) | copy-start | bytes 1540
  40.0 6.8 %copy-start.1 = (s32[32]{0:T(128)S(1)}, s32[32]{0:T(128)}, u32[]{:S(2)}) copy-start(s32[32]{0:T(128)} %param.12) | copy-start | bytes 388
  173.2 1.5 slice-start
Sparse Core Ops, SparseCore 0:
  40.2 132.9 all-reduce.1

commit v3 on v2

--- a/solution.py
+++ b/solution.py
@@ -170,7 +170,9 @@
         up = cot[pl.ds(16 * x, 16)].reshape(512, C).astype(F32)
         g = (up * sg * (1.0 + pre * (1.0 - sg)) * keep).astype(BF16)
         grad[pl.ds(16 * x, 16)] = g.reshape(16, 32, C)
-        dwt[...] += dot(g.astype(F32).T.astype(BF16), cols[...])
+        term = dot(g.astype(F32).T.astype(BF16), cols[...])
+        for t in range(28):
+            dwt[C * t : C * t + C] += term[:, C * t : C * t + C]
         return 0
 
     lax.fori_loop(0, 4, step, 0)
@@ -241,10 +243,65 @@
         coarse_grad[h] = (dot(pick, hi) + dot(pick, lo)).astype(BF16)
 
 
-def call(kernel, outs, scratch, smem, *args, collective=None):
+def sum_kernel(n_x, n_y, term, weight_grad, bias_grad, sent, got, held, onward, arrived, result,
+               send_sem, recv_sem):
+    i, j = lax.axis_index("sx"), lax.axis_index("sy")
+    part, piece = onward.shape[0], arrived.shape[1]
+    x_peers = [lax.rem(i + d, n_x) for d in range(1, n_x)]
+    y_peers = [lax.rem(j + d, n_y) for d in range(1, n_y)]
+    devices = [(p, j) for p in x_peers] + [(i, q) for q in y_peers]
+    barrier = pltpu.get_barrier_semaphore()
+    for device in devices:
+        pl.semaphore_signal(barrier, inc=1, device_id=device, device_id_type=MESH)
+    sent[...] = term[...].astype(BF16)
+    pl.semaphore_wait(barrier, len(devices))
+
+    def rows(start, size):
+        return pl.ds(pl.multiple_of(start, 16), size)
+
+    def copy(k, src, dst, device):
+        return pltpu.make_async_remote_copy(
+            src_ref=src, dst_ref=dst, send_sem=send_sem.at[k], recv_sem=recv_sem.at[k],
+            device_id=device, device_id_type=MESH)
+
+    def run(copies):
+        for c in copies:
+            c.start()
+        for c in copies:
+            c.wait_recv()
+        return copies
+
+    nx, ny = n_x - 1, n_y - 1
+    own_x, own_y = rows(i * part, part), rows(j * piece, piece)
+    first = run([copy(d, sent.at[rows(p * part, part)], got.at[d], (p, j))
+                 for d, p in enumerate(x_peers)])
+    total = term[own_x]
+    for d in range(nx):
+        total = total + got[d].astype(F32)
+    held[...] = total
+    onward[...] = total.astype(BF16)
+    second = run([copy(nx + d, onward.at[rows(q * piece, piece)], arrived.at[d], (i, q))
+                  for d, q in enumerate(y_peers)])
+    total = held[own_y]
+    for d in range(ny):
+        total = total + arrived[d].astype(F32)
+    mine = rows(i * part + j * piece, piece)
+    result[mine] = total.astype(BF16)
+    third = run([copy(nx + ny + d, result.at[mine], result.at[mine], (i, q))
+                 for d, q in enumerate(y_peers)])
+    fourth = run([copy(nx + 2 * ny + d, result.at[own_x], result.at[own_x], (p, j))
+                  for d, p in enumerate(x_peers)])
+    for t in range(27):
+        weight_grad[t] = result[C * t : C * t + C].astype(F32).T
+    bias_grad[...] = result[27 * C : 28 * C].astype(F32).T[0:8]
+    for c in first + second + third + fourth:
+        c.wait_send()
+
+
+def call(kernel, outs, scratch, smem, *args, collective=None, n_sems=8):
     vm = pl.BlockSpec(memory_space=pltpu.VMEM)
     sm = pl.BlockSpec(memory_space=pltpu.SMEM)
-    sems = [] if collective is None else [pltpu.SemaphoreType.DMA((8,))] * 2
+    sems = [] if collective is None else [pltpu.SemaphoreType.DMA((n_sems,))] * 2
     return pl.pallas_call(
         kernel,
         out_shape=[jax.ShapeDtypeStruct(s, d) for s, d in outs],
@@ -282,12 +339,14 @@
     )
     act, grad, dwt = call(
         forward_kernel,
-        [((64, bricks, C), BF16), ((64, bricks, C), BF16), ((C, 28 * C), F32)],
+        [((64, bricks, C), BF16), ((64, bricks, C), BF16), ((28 * C, C), F32)],
         [((64, 80, C), BF16), ((6, 6, 6, 32, C), BF16), ((27 * 32, 80), BF16), ((512, 28 * C), BF16)],
         (4,),
         hidden, faces, corners, nb, live_count, weight.reshape(27 * C, C), conv_bias[None], cot_t,
     )
-    dwt = lax.psum(dwt, ("sx", "sy"))
+    unit = 16 * n_x * n_y
+    rows = -(-28 * C // unit) * unit
+    dwt = jnp.pad(dwt, ((0, rows - 28 * C), (0, 0)))
     own, faces, corners = call(
         backward_kernel, [((64, bricks, C), F32), pack_f, pack_c],
         [((6, 6, 6, 32, C), F32), ((27 * 32, 80), BF16), ((64, 40, C), F32)], (),
@@ -300,6 +359,14 @@
         own, faces, corners, child_code[None], face_idx[None], corner_idx[None],
         collective=1,
     )
+    part, piece = rows // n_x, rows // (n_x * n_y)
+    weight_grad, bias_grad = call(
+        functools.partial(sum_kernel, n_x, n_y),
+        [((27, C, C), F32), ((8, C), F32)],
+        [((rows, C), BF16), ((n_x - 1, part, C), BF16), ((part, C), F32), ((part, C), BF16),
+         ((n_y - 1, piece, C), BF16), ((rows, C), BF16)],
+        (), dwt, collective=2, n_sems=2 * (n_x + n_y - 2),
+    )
     coarse_grad = (
         coarse_grad.reshape(2, 2, 2, 2, 2, 2, parents, C)
         .transpose(6, 3, 0, 4, 1, 5, 2, 7)
@@ -309,8 +376,8 @@
         act.transpose(1, 0, 2),
         skip_grad.transpose(1, 0, 2),
         coarse_grad,
-        dwt[:, : 27 * C].reshape(C, 27, C).transpose(1, 2, 0),
-        dwt[:, 27 * C],
+        weight_grad,
+        bias_grad[0],
     )
 
 

time: 187 us -> 90.5 us (0.48); the launches traced: 185 us -> 90.2 us
  waiting for transfers between devices: 110 us -> 0 us
  Pallas kernels: 45.2 us -> 77.5 us
  between operations: 14.8 us -> 1.46 us
  local copies, waits for them, and re-layouts: 13.3 us -> 10.4 us
    psum x1 -> x0, waiting for transfers between devices: 110 us -> none  [local(): dwt = lax.psum(dwt, ('sx', 'sy'))]
    pallas_call x4 -> x5, Pallas kernels: 45.2 us -> 77.5 us  [call(): pl.pallas_call(kernel, out_shape=[jax.ShapeDtypeStruct(s, d) for s, d in...]
    slice x4 -> x0, local copies, waits for them, and re-layouts: 4.63 us -> none  [the longest x3 3.16 us: local(): dwt[:, :27 * C].reshape(C, 27, C).transpose(1, 2, 0)]
    unnamed x12 -> x13, local copies, waits for them, and re-layouts: 3.75 us -> 4.95 us
  transfers between devices with their start and end apart: 1 -> 0, of which waited for: 1 -> 0; matrix products, arithmetic and copies ran while one was open for 2% -> 0% of each run, Pallas kernels for 11% -> 0%
where the time goes in v3:
time: 90.5 us; the launch traced here: 90.2 us
  Pallas kernels  77.5 us (86%)
  local copies, waits for them, and re-layouts  10.4 us (11%)
  between operations  1.46 us (2%)
    pallas_call x5, Pallas kernels, call(): pl.pallas_call(kernel, out_shape=[jax.ShapeDtypeStruct(s, d) for s, d in...  77.5 us
    unnamed x13, local copies, waits for them, and re-layouts  4.95 us

profile of v3, /device:TPU:1, one launch (start us, length us, event | category | flops | bytes accessed | tf_op | source)
XLA Modules:
  0.0 90.2 jit_solution(8116062340499217466)
XLA Ops:
  1.4 0.8 copy.28
  2.1 0.8 broadcast_add_fusion.1
  2.9 0.1 add.80.face_idx
  3.0 0.1 broadcast_add_fusion
  3.0 0.1 add.81.corner_idx
  3.2 0.1 add.83.corner_idx
  3.2 0.8 copy.32
  4.0 0.7 copy.29.child
  4.8 0.1 add.82.face_idx
  4.9 1.1 %copy.27 = bf16[8,2,2,2,2,2,2,128]{7,0,5,3,1,6,4,2:T(8,128)(2,1)S(1)} copy(bf16[8,2,2,2,2,2,2,128]{7,6,5,4,3,2,1,0:T(2,128)(2,1)} %bitcast.35) | data formatting | bytes 262144 | tf_op jit(solution)/shard_map/reshape | solution.py:326
  5.9 0.5 reshape.134.nb
  6.4 1.4 %copy.42 = bf16[32,64,128]{2,0,1:T(8,128)(2,1)S(1)} copy(bf16[32,64,128]{2,1,0:T(8,128)(2,1)} %param.10) | data formatting | bytes 1048576 | tf_op args[0]
  7.8 12.3 %shard_map.137 = (bf16[64,32,128]{2,1,0:T(8,128)(2,1)S(1)}, bf16[4,32,16,128]{3,2,1,0:T(8,128)(2,1)S(1)}, bf16[4,8,16,128]{3,2,1,0:T(8,128)(2,1)S(1)}) custom-call(bf16[64,32,128]{2,1,0:T(8,128)(2,1)S(1)} %bitcast.26, bf16[8,64,128]{2,1,0:T(8,128)(2,1)S(1)} %bitcast.28, s32[32,1]{1,0:T(8,128)S(1)} %copy.29.child, s32[1]{0:T(128)S(6)} %copy.44.live, ...), custom_call_target="tpu_custom_call" | custom-call | tf_op jit(solution)/shard_map/pallas_call | solution.py:305
  20.1 0.3 copy.41
  20.4 12.1 %shard_map.138 = (bf16[64,32,128]{2,1,0:T(8,128)(2,1)S(1)}, bf16[64,32,128]{2,1,0:T(8,128)(2,1)S(1)}, f32[3584,128]{1,0:T(8,128)S(1)}) custom-call(bf16[64,32,128]{2,1,0:T(8,128)(2,1)S(1)} %get-tuple-element.18.hidden, bf16[4,32,16,128]{3,2,1,0:T(8,128)(2,1)S(1)} %get-tuple-element.19.faces, bf16[4,8,16,128]{3,2,1,0:T(8,128)(2,1)S(1)} %get-tuple-element.20.corners, ...), custom_call_target="tpu_custom_call" | custom-call | tf_op jit(solution)/shard_map/pallas_call | solution.py:305
  32.5 0.0 copy-start.1
  32.5 1.0 %copy.37 = bf16[32,64,128]{2,1,0:T(8,128)(2,1)} copy(bf16[32,64,128]{2,0,1:T(8,128)(2,1)S(1)} %bitcast.29) | data formatting | bytes 1048576
  33.5 5.6 %shard_map.139 = (f32[64,32,128]{2,1,0:T(8,128)S(1)}, bf16[4,32,16,128]{3,2,1,0:T(8,128)(2,1)S(1)}, bf16[4,8,16,128]{3,2,1,0:T(8,128)(2,1)S(1)}) custom-call(bf16[64,32,128]{2,1,0:T(8,128)(2,1)S(1)} %get-tuple-element.22.grad, s32[864,1]{1,0:T(8,128)S(1)} %reshape.134.nb, bf16[27,128,128]{2,1,0:T(8,128)(2,1)S(1)} %copy-done), custom_call_target="tpu_custom_call" | custom-call | tf_op jit(solution)/shard_map/pallas_call | solution.py:305
  39.2 12.1 %shard_map.140 = (bf16[64,32,128]{2,1,0:T(8,128)(2,1)S(1)}, bf16[8,64,128]{2,1,0:T(8,128)(2,1)S(1)}) custom-call(f32[64,32,128]{2,1,0:T(8,128)S(1)} %get-tuple-element.23.own, bf16[4,32,16,128]{3,2,1,0:T(8,128)(2,1)S(1)} %get-tuple-element.24.sent_faces, bf16[4,8,16,128]{3,2,1,0:T(8,128)(2,1)S(1)} %get-tuple-element.25.sent_corners, s32[1,32]{1,0:T(1,128)S(1)} %bitcast.33, ...), custom_call_target="tpu_custom_call" | custom-call | tf_op jit(solution)/shard_map/pallas_call | solution.py:305
  51.3 1.0 %copy.38 = bf16[32,64,128]{2,1,0:T(8,128)(2,1)} copy(bf16[32,64,128]{2,0,1:T(8,128)(2,1)S(1)} %bitcast.30) | data formatting | bytes 1048576
  52.3 0.8 copy.36
  53.1 35.4 %shard_map.141 = (f32[27,128,128]{2,1,0:T(8,128)S(1)}, f32[8,128]{1,0:T(8,128)S(1)}) custom-call(f32[3584,128]{1,0:T(8,128)S(1)} %get-tuple-element.28.term), custom_call_target="tpu_custom_call" | custom-call | tf_op jit(solution)/shard_map/pallas_call | solution.py:305
  88.5 0.5 slice_bitcast_fusion
  89.0 1.2 %copy.45 = f32[27,128,128]{2,1,0:T(8,128)} copy(f32[27,128,128]{2,1,0:T(8,128)S(1)} %get-tuple-element.49) | data formatting | bytes 3538944
  (9 shorter events, 0.0 us)
Async XLA Ops:
  0.6 19.4 %copy-start.3 = (bf16[32,64,128]{2,1,0:T(8,128)(2,1)S(1)}, bf16[32,64,128]{2,1,0:T(8,128)(2,1)}, u32[]{:S(2)}) copy-start(bf16[32,64,128]{2,1,0:T(8,128)(2,1)} %param.19) | copy-start | bytes 1572868
  4.8 15.6 %copy-start = (bf16[27,128,128]{2,1,0:T(8,128)(2,1)S(1)}, bf16[27,128,128]{2,1,0:T(8,128)(2,1)}, u32[]{:S(2)}) copy-start(bf16[27,128,128]{2,1,0:T(8,128)(2,1)} %weight.1) | copy-start | bytes 2654212
  4.8 15.6 %copy-start.2 = (f32[128]{0:T(128)S(1)}, f32[128]{0:T(128)}, u32[]{:S(2)}) copy-start(f32[128]{0:T(128)} %param.18) | copy-start | bytes 1540
  32.5 6.6 %copy-start.1 = (s32[32]{0:T(128)S(1)}, s32[32]{0:T(128)}, u32[]{:S(2)}) copy-start(s32[32]{0:T(128)} %param.12) | copy-start | bytes 388
